TPU v7x, 256 devices: a whole 4x4x8 slice. The times are simulated.
256 devices in a mesh: rows: 256 (over y, x, z, core).
Axes of the slice: x: 4, y: 4, z: 8, core: 2. Of those that a mesh axis runs over, the one named last changes fastest.
Arguments:
- velocity: bfloat16 [131072, 8192], P('rows'), as said below
- basis_in: bfloat16 [131072, 256], P('rows'), may hold values from -0.015625 to 0.015625
Outputs:
- basis_out: float32 [131072, 256], P('rows')
- r_factor: float32 [256, 256], replicated
Inputs may be any that keep to these rules, and one draw needn't show every extreme that they name: Entries of the velocity record lie within -15 and 15.
All inputs are finite; a program needn't handle non-finite values.
Results may differ from a plain program's by a relative error of at most 0.0029.
Values may be sent and summed in bfloat16 or wider, within the bound.
A program may use at most 128 MiB of HBM per device.

v0:
```python
import jax
import jax.numpy as jnp
from jax import lax
from jax.sharding import PartitionSpec as P


def from_partner(value, axis, apart):
    mask = 2**apart
    pairs = [(source, source ^ mask) for source in range(lax.axis_size(axis))]
    return lax.ppermute(value, axis, pairs)


def gram_of(matrix):
    return lax.dot_general(
        matrix,
        matrix,
        (((0,), (0,)), ((), ())),
        precision=lax.Precision.HIGHEST,
        preferred_element_type=jnp.float32,
    )


def triangle(gram_matrix):
    return jnp.linalg.cholesky(gram_matrix).T


def right_divide(matrix, r_factor):
    return jax.scipy.linalg.solve_triangular(r_factor.T, matrix.T, lower=True).T


def upper_half(matrix):
    return jnp.triu(matrix, 1) + jnp.diag(0.5 * jnp.diagonal(matrix))


def near_identity_factor(gram_matrix):
    width = gram_matrix.shape[0]
    excess = gram_matrix - jnp.eye(width, dtype=jnp.float32)
    upper_part = jnp.zeros_like(excess)
    for sweep in range(3):
        square_part = jnp.dot(upper_part.T, upper_part, precision=lax.Precision.HIGHEST)
        upper_part = upper_half(excess - square_part)
    return jnp.eye(width, dtype=jnp.float32) + upper_part


def cholqr_twice(matrix):
    first_r = triangle(gram_of(matrix))
    once_done = right_divide(matrix, first_r)
    second_r = near_identity_factor(gram_of(once_done))
    return jnp.dot(second_r, first_r, precision=lax.Precision.HIGHEST)


def local(velocity, basis_in):
    rows_here = velocity.shape[0]
    devices = lax.axis_size("rows")
    partial_sum = lax.dot_general(
        velocity, basis_in, (((0,), (0,)), ((), ())), preferred_element_type=jnp.float32
    )
    coefficients = lax.psum(partial_sum, "rows").astype(jnp.bfloat16)
    projected = jnp.dot(velocity, coefficients, preferred_element_type=jnp.float32)
    r_factor = cholqr_twice(projected)
    my_index = lax.axis_index("rows")
    for level in range(devices.bit_length() - 1):
        partner = from_partner(r_factor, "rows", level)
        low_side = my_index // (1 << level) % 2 == 0
        top_part = jnp.where(low_side, r_factor, partner)
        bottom_part = jnp.where(low_side, partner, r_factor)
        r_factor = cholqr_twice(jnp.concatenate([top_part, bottom_part], 0))
    norm_scale = jnp.sqrt(jnp.float32(devices * rows_here))
    basis_out = right_divide(projected, r_factor) * norm_scale
    return (basis_out, r_factor / norm_scale)


def solution(mesh):
    in_specs = (P("rows", None), P("rows", None))
    out_specs = (P("rows", None), P())
    return jax.shard_map(local, mesh=mesh, in_specs=in_specs, out_specs=out_specs, check_vma=False)
```

profile of v0, /device:TPU:1, one launch (start us, length us, event | category | flops | bytes accessed | tf_op | source)
XLA Modules:
  0.0 917.8 jit_solution(9953126451125474481)
XLA Ops:
  10.6 147.5 %all-reduce.2 = bf16[8192,256]{1,0:T(8,128)(2,1)} all-reduce(f32[8192,256]{1,0:T(8,128)} %fusion.396), channel_id=1, replica_groups=mesh['rows'=256] {'rows'}, use_global_device_ids=true, to_apply=%region_0.0 | all-reduce | flops 2097152 | bytes 12582912 | tf_op jit(solution)/shard_map/psum | solution.py:58
  166.0 11.7 %cholesky.424 = f32[128,128]{1,0:T(8,128)S(1)} custom-call(f32[128,128]{1,0:T(8,128)S(1)} %cholesky.726), custom_call_target="Cholesky" | custom-call | tf_op jit(solution)/shard_map/jit(cholesky)/cholesky | solution.py:24
  188.0 11.9 %cholesky.441 = f32[128,128]{1,0:T(8,128)S(1)} custom-call(f32[128,128]{1,0:T(8,128)S(1)} %convolution_subtract_fusion.28), custom_call_target="Cholesky" | custom-call | tf_op jit(solution)/shard_map/jit(cholesky)/cholesky | solution.py:24
  206.2 19.7 %custom-call.83 = f32[2,128,128]{1,2,0:T(8,128)S(1)} custom-call(f32[2,128,128]{2,1,0:T(8,128)S(1)} %get-tuple-element.66), custom_call_target="InvertDiagBlocksLowerTriangular" | custom-call | tf_op jit(solution)/shard_map/jit(_solve_triangular)/triangular_solve | solution.py:28
  242.4 11.7 %cholesky.458 = f32[128,128]{1,0:T(8,128)S(1)} custom-call(f32[128,128]{1,0:T(8,128)S(1)} %cholesky.729), custom_call_target="Cholesky" | custom-call | tf_op jit(solution)/shard_map/jit(cholesky)/cholesky | solution.py:24
  264.4 11.7 %cholesky.475 = f32[128,128]{1,0:T(8,128)S(1)} custom-call(f32[128,128]{1,0:T(8,128)S(1)} %convolution_subtract_fusion.27), custom_call_target="Cholesky" | custom-call | tf_op jit(solution)/shard_map/jit(cholesky)/cholesky | solution.py:24
  283.1 19.7 %custom-call.85 = f32[2,128,128]{1,2,0:T(8,128)S(1)} custom-call(f32[2,128,128]{2,1,0:T(8,128)S(1)} %get-tuple-element.67), custom_call_target="InvertDiagBlocksLowerTriangular" | custom-call | tf_op jit(solution)/shard_map/jit(_solve_triangular)/triangular_solve | solution.py:28
  344.9 11.7 %cholesky.509 = f32[128,128]{1,0:T(8,128)S(1)} custom-call(f32[128,128]{1,0:T(8,128)S(1)} %convolution_subtract_fusion.26), custom_call_target="Cholesky" | custom-call | tf_op jit(solution)/shard_map/jit(cholesky)/cholesky | solution.py:24
  363.8 19.7 %custom-call.87 = f32[2,128,128]{1,2,0:T(8,128)S(1)} custom-call(f32[2,128,128]{2,1,0:T(8,128)S(1)} %get-tuple-element.68), custom_call_target="InvertDiagBlocksLowerTriangular" | custom-call | tf_op jit(solution)/shard_map/jit(_solve_triangular)/triangular_solve | solution.py:28
  395.3 14.0 %collective-permute-done.2 = f32[256,256]{1,0:T(8,128)S(1)} collective-permute-done((f32[256,256]{1,0:T(8,128)S(1)}, f32[256,256]{1,0:T(8,128)S(1)}, u32[]{:S(2)}, u32[]{:S(2)}) %collective-permute-start.2) | collective-permute-done | bytes 262176 | tf_op jit(solution)/shard_map/ppermute | solution.py:10
  432.7 11.7 %cholesky.543 = f32[128,128]{1,0:T(8,128)S(1)} custom-call(f32[128,128]{1,0:T(8,128)S(1)} %convolution_subtract_fusion.25), custom_call_target="Cholesky" | custom-call | tf_op jit(solution)/shard_map/jit(cholesky)/cholesky | solution.py:24
  451.4 19.7 %custom-call.89 = f32[2,128,128]{1,2,0:T(8,128)S(1)} custom-call(f32[2,128,128]{2,1,0:T(8,128)S(1)} %get-tuple-element.69), custom_call_target="InvertDiagBlocksLowerTriangular" | custom-call | tf_op jit(solution)/shard_map/jit(_solve_triangular)/triangular_solve | solution.py:28
  484.0 14.7 %collective-permute-done.3 = f32[256,256]{1,0:T(8,128)S(1)} collective-permute-done((f32[256,256]{1,0:T(8,128)S(1)}, f32[256,256]{1,0:T(8,128)S(1)}, u32[]{:S(2)}, u32[]{:S(2)}) %collective-permute-start.3) | collective-permute-done | bytes 262176 | tf_op jit(solution)/shard_map/ppermute | solution.py:10
  522.1 11.7 %cholesky.577 = f32[128,128]{1,0:T(8,128)S(1)} custom-call(f32[128,128]{1,0:T(8,128)S(1)} %convolution_subtract_fusion.24), custom_call_target="Cholesky" | custom-call | tf_op jit(solution)/shard_map/jit(cholesky)/cholesky | solution.py:24
  540.7 19.7 %custom-call.91 = f32[2,128,128]{1,2,0:T(8,128)S(1)} custom-call(f32[2,128,128]{2,1,0:T(8,128)S(1)} %get-tuple-element.70), custom_call_target="InvertDiagBlocksLowerTriangular" | custom-call | tf_op jit(solution)/shard_map/jit(_solve_triangular)/triangular_solve | solution.py:28
  602.4 11.7 %cholesky.611 = f32[128,128]{1,0:T(8,128)S(1)} custom-call(f32[128,128]{1,0:T(8,128)S(1)} %convolution_subtract_fusion.23), custom_call_target="Cholesky" | custom-call | tf_op jit(solution)/shard_map/jit(cholesky)/cholesky | solution.py:24
  621.3 19.7 %custom-call.93 = f32[2,128,128]{1,2,0:T(8,128)S(1)} custom-call(f32[2,128,128]{2,1,0:T(8,128)S(1)} %get-tuple-element.71), custom_call_target="InvertDiagBlocksLowerTriangular" | custom-call | tf_op jit(solution)/shard_map/jit(_solve_triangular)/triangular_solve | solution.py:28
  683.5 11.7 %cholesky.645 = f32[128,128]{1,0:T(8,128)S(1)} custom-call(f32[128,128]{1,0:T(8,128)S(1)} %convolution_subtract_fusion.22), custom_call_target="Cholesky" | custom-call | tf_op jit(solution)/shard_map/jit(cholesky)/cholesky | solution.py:24
  702.2 19.7 %custom-call.95 = f32[2,128,128]{1,2,0:T(8,128)S(1)} custom-call(f32[2,128,128]{2,1,0:T(8,128)S(1)} %get-tuple-element.72), custom_call_target="InvertDiagBlocksLowerTriangular" | custom-call | tf_op jit(solution)/shard_map/jit(_solve_triangular)/triangular_solve | solution.py:28
  761.8 11.7 %cholesky.679 = f32[128,128]{1,0:T(8,128)S(1)} custom-call(f32[128,128]{1,0:T(8,128)S(1)} %convolution_subtract_fusion.21), custom_call_target="Cholesky" | custom-call | tf_op jit(solution)/shard_map/jit(cholesky)/cholesky | solution.py:24
  780.5 19.7 %custom-call.97 = f32[2,128,128]{1,2,0:T(8,128)S(1)} custom-call(f32[2,128,128]{2,1,0:T(8,128)S(1)} %get-tuple-element.73), custom_call_target="InvertDiagBlocksLowerTriangular" | custom-call | tf_op jit(solution)/shard_map/jit(_solve_triangular)/triangular_solve | solution.py:28
  841.5 11.7 %cholesky.713 = f32[128,128]{1,0:T(8,128)S(1)} custom-call(f32[128,128]{1,0:T(8,128)S(1)} %convolution_subtract_fusion.20), custom_call_target="Cholesky" | custom-call | tf_op jit(solution)/shard_map/jit(cholesky)/cholesky | solution.py:24
  859.9 19.7 %custom-call.99 = f32[2,128,128]{1,2,0:T(8,128)S(1)} custom-call(f32[2,128,128]{2,1,0:T(8,128)S(1)} %get-tuple-element.74), custom_call_target="InvertDiagBlocksLowerTriangular" | custom-call | tf_op jit(solution)/shard_map/jit(_solve_triangular)/triangular_solve | solution.py:28
  894.8 19.7 %custom-call.100 = f32[2,128,128]{1,2,0:T(8,128)S(1)} custom-call(f32[2,128,128]{2,1,0:T(8,128)S(1)} %get-tuple-element.75), custom_call_target="InvertDiagBlocksLowerTriangular" | custom-call | tf_op jit(solution)/shard_map/jit(_solve_triangular)/triangular_solve | solution.py:28
  (369 shorter events, 441.9 us)
Async XLA Ops:
  0.6 1.0 copy-start
  236.5 4.5 collective-permute-start
  313.6 7.8 collective-permute-start.1
  394.3 15.0 %collective-permute-start.2 = (f32[256,256]{1,0:T(8,128)S(1)}, f32[256,256]{1,0:T(8,128)S(1)}, u32[]{:S(2)}, u32[]{:S(2)}) collective-permute-start(f32[256,256]{1,0:T(8,128)S(1)} %fusion.48), channel_id=1, source_target_pairs={{0,4},{1,5},{2,6},{3,7},{4,0},{5,1},{6,2},{7,3},{8,12},{9,13},{10,... | collective-permute-start | bytes 786440 | tf_op jit(solution)/shard_map/ppermute | solution.py:10
  481.9 16.7 %collective-permute-start.3 = (f32[256,256]{1,0:T(8,128)S(1)}, f32[256,256]{1,0:T(8,128)S(1)}, u32[]{:S(2)}, u32[]{:S(2)}) collective-permute-start(f32[256,256]{1,0:T(8,128)S(1)} %fusion.49), channel_id=1, source_target_pairs={{0,8},{1,9},{2,10},{3,11},{4,12},{5,13},{6,14},{7,15},{8,0},{9,1},... | collective-permute-start | bytes 786440 | tf_op jit(solution)/shard_map/ppermute | solution.py:10
  571.3 7.7 collective-permute-start.4
  651.8 8.2 collective-permute-start.5
  732.7 5.7 collective-permute-start.6
  811.0 7.0 collective-permute-start.7
  855.7 61.8 %copy-start.1 = (bf16[512,256]{1,0:T(8,128)(2,1)S(1)}, bf16[512,256]{1,0:T(8,128)(2,1)}, u32[]{:S(2)}) copy-start(bf16[512,256]{1,0:T(8,128)(2,1)} %param.6) | copy-start | bytes 786436
where the time goes:
time: 925 us; the launch traced here: 918 us
  other arithmetic  510 us (55%)
  blocking collectives  148 us (16%)
  local copies, waits for them, and re-layouts  107 us (12%)
  matrix products  63.9 us (7%)
  waiting for transfers between devices  62.3 us (7%)
  between operations  14.1 us (2%)
  starting transfers between devices  10.2 us (1%)
    another operation x62, other arithmetic, triangle(): return jnp.linalg.cholesky(gram_matrix).T  311 us
    another operation x20, other arithmetic, right_divide(): return jax.scipy.linalg.solve_triangular(r_factor.T, matrix.T, lower=True).T  197 us
    psum x1, blocking collectives, local(): coefficients = lax.psum(partial_sum, 'rows').astype(jnp.bfloat16)  148 us
    gather x27, local copies, waits for them, and re-layouts, upper_half(): return jnp.triu(matrix, 1) + jnp.diag(0.5 * jnp.diagonal(matrix))  63.3 us
    ppermute x8, waiting for transfers between devices, from_partner(): return lax.ppermute(value, axis, pairs)  62.3 us
    another operation x75, local copies, waits for them, and re-layouts, right_divide(): return jax.scipy.linalg.solve_triangular(r_factor.T, matrix.T, lower=True).T  40.4 us
  transfers between devices with their start and end apart: 8, of which 8 were waited for; matrix products, arithmetic and copies ran while one was open for 0% of the time, Pallas kernels for 0%

commit v1 on v0

v1 whole, which is shorter than its diff:
```python
import functools

import jax
import jax.numpy as jnp
from jax import lax
from jax.experimental import pallas as pl
from jax.experimental.pallas import tpu as pltpu
from jax.sharding import PartitionSpec as P

NY, NX, NZ = 4, 4, 8
SIZE = {"x": NX, "z": NZ, "y": NY}
PLACE = {"x": 0, "z": 1, "y": 2}
MESH = pl.DeviceIdType.MESH
HIGHEST = lax.Precision.HIGHEST

RS_PARTS = ((0, 24, "xyz"), (24, 24, "yzx"), (48, 16, "zxy"))
AG_PARTS = ((0, 32, "zyx"), (32, 16, "xzy"), (48, 16, "yxz"))


def dot(a, b, contract, precision=None):
    return lax.dot_general(
        a, b, ((contract[:1], contract[1:]), ((), ())),
        precision=precision, preferred_element_type=jnp.float32,
    )


def block_of(at, first, rows, full, fixed, split=None):
    index = [None, None, None]
    for axis in "xzy":
        place = PLACE[axis]
        if axis in fixed:
            index[place] = pl.ds(fixed[axis], 1)
        else:
            index[place] = pl.ds(0, SIZE[axis])
    if split is not None and split[0] == "row":
        first, rows = first + split[1], split[2]
    elif split is not None:
        index[PLACE[split[0]]] = pl.ds(split[1], split[2])
    return at[tuple(index) + (pl.ds(first, rows), slice(None))]


def halves_of(rows, whole_axes, granule):
    if whole_axes:
        axis = whole_axes[0]
        half = SIZE[axis] // 2
        return ((axis, 0, half), (axis, half, half))
    if rows >= 2 * granule:
        upper = rows // 2 // granule * granule
        return (("row", 0, upper), ("row", upper, rows - upper))
    return (("row", 0, rows), None)


def block_shape(rows, whole_axes, split):
    shape = [1, 1, 1]
    for axis in whole_axes:
        shape[PLACE[axis]] = SIZE[axis]
    if split is not None and split[0] == "row":
        rows = split[2]
    elif split is not None:
        shape[PLACE[split[0]]] = split[2]
    return tuple(shape) + (rows, 128)


def rs_messages():
    messages = []
    for part, (first, rows, order) in enumerate(RS_PARTS):
        for stage, axis in enumerate(order):
            rest = order[stage + 1:]
            halves = halves_of(rows, rest, 8)
            for step in range(1, SIZE[axis] // 2 + 1):
                for way in (0, 1):
                    split = halves[way] if step == 1 else None
                    messages.append(((part, stage, step, way), block_shape(rows, rest, split)))
    return messages


RS_MESSAGES = rs_messages()
RS_SLOT = {key: slot for slot, (key, _) in enumerate(RS_MESSAGES)}
N_RS = len(RS_MESSAGES)
N_AG = 64
N_SIB = 64


def exchange_kernel(*refs):
    v_hbm, b_hbm, p_ref, g_ref = refs[:4]
    (v, v_sib, b, b_sib, total, gathered, gram_in, gram_chip, gram_parts, gram_z, gram_row) = refs[4:15]
    received = refs[15:15 + N_RS]
    (load_sem, sib_send, sib_recv, rs_send, rs_recv, ag_send, ag_recv,
     fwd_send, fwd_recv, gx_send, gx_recv) = refs[15 + N_RS:]

    me = lax.axis_index("rows")
    core = me % 2
    mine = {"z": me // 2 % NZ, "x": me // (2 * NZ) % NX, "y": me // (2 * NZ * NX)}

    def device(**moved):
        at = {**mine, "core": core, **moved}
        return (((at["y"] * NX + at["x"]) * NZ + at["z"]) * 2 + at["core"],)

    def along(axis, offset):
        return (mine[axis] + offset + SIZE[axis]) % SIZE[axis]

    sibling = device(core=1 - core)

    def remote(source, target, send, recv, to):
        return pltpu.make_async_remote_copy(
            src_ref=source, dst_ref=target, send_sem=send, recv_sem=recv,
            device_id=to, device_id_type=MESH,
        )

    half = v_sib.shape[1]
    wide = half // NX

    def columns(which_core, k):
        return pl.ds(pl.multiple_of(which_core * half + k * wide, 128), wide)

    loads = []
    for n, (which, k) in enumerate([(core, k) for k in range(NX)] + [(1 - core, k) for k in range(NX)]):
        loads.append(pltpu.make_async_copy(
            v_hbm.at[:, columns(which, k)], v.at[:, columns(which, k)], load_sem.at[n]))
    load_b = pltpu.make_async_copy(b_hbm, b, load_sem.at[2 * NX])
    load_b.start()
    for load in loads:
        load.start()

    partners = [sibling]
    for dy in range(NY):
        for dx in range(NX):
            if dy or dx:
                partners.append(device(y=along("y", dy), x=along("x", dx)))
    for dz in range(1, NZ):
        partners.append(device(z=along("z", dz)))
    barrier = pltpu.get_barrier_semaphore()
    for partner in partners:
        pl.semaphore_signal(barrier, inc=1, device_id=partner, device_id_type=MESH)
    pl.semaphore_wait(barrier, len(partners))

    sends = []

    copy_b = remote(b_hbm, b_sib, sib_send.at[NX], sib_recv.at[NX], sibling)
    copy_b.start()
    copies_v = []
    for k in range(NX):
        copy = remote(
            v_hbm.at[:, columns(1 - core, k)], v_sib.at[:, pl.ds(k * wide, wide)],
            sib_send.at[k], sib_recv.at[k], sibling)
        copy.start()
        copies_v.append(copy)
    sends += copies_v + [copy_b]

    load_b.wait()
    copy_b.wait_recv()
    b_t = b[...].T
    b_sib_t = b_sib[...].T
    for k in range(NX):
        loads[k].wait()
        copies_v[k].wait_recv()
        product = dot(b_t, v[:, columns(core, k)], (1, 0))
        product += dot(b_sib_t, v_sib[:, k * wide:(k + 1) * wide], (1, 0))
        for n in range(NZ):
            total[k, n] = product[:, n * 128:(n + 1) * 128].reshape(NY, 64, 128)

    def rs_block(part, stage, target, split=None):
        first, rows, order = RS_PARTS[part]
        axis = order[stage]
        fixed = {done: mine[done] for done in order[:stage]}
        fixed[axis] = target
        return block_of(total.at, first, rows, order[stage + 1:], fixed, split)

    def rs_copy(part, stage, step, way):
        first, rows, order = RS_PARTS[part]
        axis = order[stage]
        sign = 1 - 2 * way
        target = along(axis, sign * (SIZE[axis] // 2 - step + 1))
        split = halves_of(rows, order[stage + 1:], 8)[way] if step == 1 else None
        slot = RS_SLOT[part, stage, step, way]
        return remote(
            rs_block(part, stage, target, split), received[slot], rs_send.at[slot], rs_recv.at[slot],
            device(**{axis: along(axis, sign)}))

    def rs_start(part, stage, step):
        for way in (0, 1):
            copy = rs_copy(part, stage, step, way)
            copy.start()
            sends.append(copy)

    def rs_finish(part, stage, step):
        first, rows, order = RS_PARTS[part]
        axis = order[stage]
        for way in (0, 1):
            sign = 1 - 2 * way
            slot = RS_SLOT[part, stage, step, way]
            rs_copy(part, stage, step, way).wait_recv()
            target = along(axis, sign * (SIZE[axis] // 2 - step))
            split = halves_of(rows, order[stage + 1:], 8)[way] if step == 1 else None
            block = rs_block(part, stage, target, split)
            block[...] = block[...] + received[slot][...]

    steps = []
    for first, rows, order in RS_PARTS:
        steps.append([(stage, step) for stage, axis in enumerate(order) for step in range(1, SIZE[axis] // 2 + 1)])
    for part in (0, 1, 2):
        rs_start(part, *steps[part][0])
    for turn in range(len(steps[0])):
        for part in (2, 0, 1):
            rs_finish(part, *steps[part][turn])
            if turn + 1 < len(steps[part]):
                rs_start(part, *steps[part][turn + 1])

    own = total[pl.ds(mine["x"], 1), pl.ds(mine["z"], 1), pl.ds(mine["y"], 1)]
    gathered[pl.ds(core, 1), pl.ds(mine["x"], 1), pl.ds(mine["z"], 1), pl.ds(mine["y"], 1)] = (
        own.astype(jnp.bfloat16)[None])

    def ag_block(part, stage, origin, split=None, whole_stage=False):
        first, rows, order = AG_PARTS[part]
        axis = order[stage]
        fixed = {later: mine[later] for later in order[stage + 1:]}
        if not whole_stage:
            fixed[axis] = origin
        return block_of(gathered.at[core].at, first, rows, order[:stage], fixed, split)

    counters = {"ag": 0, "fwd": 0}

    def forward(ref):
        slot = counters["fwd"]
        counters["fwd"] += 1
        copy = remote(ref, ref, fwd_send.at[slot], fwd_recv.at[slot], sibling)
        copy.start()
        sends.append(copy)
        return slot

    def sibling_block(part, stage, origin, split):
        first, rows, order = AG_PARTS[part]
        axis = order[stage]
        fixed = {axis: origin}
        return block_of(gathered.at[1 - core].at, first, rows, order[:stage], fixed, split)

    forwarded = []
    pending = {}

    def ag_start(part, stage, step):
        first, rows, order = AG_PARTS[part]
        axis = order[stage]
        last = step == SIZE[axis] // 2
        halves = halves_of(rows, order[:stage], 16)
        if stage == 2 and step == 1:
            slot = forward(ag_block(part, stage, mine[axis]))
            forwarded.append((slot, part, stage, mine[axis], None))
        for way in (0, 1):
            sign = 1 - 2 * way
            split = halves[way] if last else None
            if last and split is None:
                continue
            block = ag_block(part, stage, along(axis, -sign * (step - 1)), split)
            slot = counters["ag"]
            counters["ag"] += 1
            copy = remote(block, block, ag_send.at[slot], ag_recv.at[slot], device(**{axis: along(axis, sign)}))
            copy.start()
            sends.append(copy)
            arriving = ag_block(part, stage, along(axis, -sign * step), split)
            pending[part, stage, step, way] = (slot, arriving, along(axis, -sign * step), split)

    def ag_finish(part, stage, step):
        first, rows, order = AG_PARTS[part]
        axis = order[stage]
        for way in (0, 1):
            if (part, stage, step, way) not in pending:
                continue
            slot, arriving, origin, split = pending[part, stage, step, way]
            remote(arriving, arriving, ag_send.at[slot], ag_recv.at[slot], sibling).wait_recv()
            if stage == 2:
                slot = forward(arriving)
                forwarded.append((slot, part, stage, origin, split))

    steps = []
    for first, rows, order in AG_PARTS:
        steps.append([(stage, step) for stage, axis in enumerate(order) for step in range(1, SIZE[axis] // 2 + 1)])
    for part in (0, 1, 2):
        ag_start(part, *steps[part][0])
    for turn in range(len(steps[0])):
        for part in (0, 1, 2):
            ag_finish(part, *steps[part][turn])
            if turn + 1 < len(steps[part]):
                ag_start(part, *steps[part][turn + 1])
    for slot, part, stage, origin, split in forwarded:
        block = sibling_block(part, stage, origin, split)
        remote(block, block, fwd_send.at[slot], fwd_recv.at[slot], sibling).wait_recv()

    for load in loads[NX:]:
        load.wait()
    projected = None
    for which in range(2):
        for k in range(NX):
            block = jnp.concatenate([gathered[which, k, n].reshape(256, 128) for n in range(NZ)], axis=1)
            term = dot(v[:, which * half + k * wide:which * half + (k + 1) * wide], block, (1, 1))
            projected = term if projected is None else projected + term
    p_ref[...] = projected
    gram_in[0] = dot(projected, projected, (0, 0), HIGHEST)

    copy = remote(gram_in.at[0], gram_in.at[1], gx_send.at[0], gx_recv.at[0], sibling)
    copy.start()
    sends.append(copy)
    copy.wait_recv()
    gram_chip[...] = (gram_in[0] + gram_in[1]).reshape(2, NY, NX, 8, 256)

    plane = [(dy, dx) for dy in range(NY) for dx in range(NX) if dy or dx]
    scatter = []
    for n, (dy, dx) in enumerate(plane):
        y, x = along("y", dy), along("x", dx)
        copy = remote(
            gram_chip.at[core, y, x], gram_parts.at[n], gx_send.at[1 + n], gx_recv.at[1 + n], device(y=y, x=x))
        copy.start()
        scatter.append(copy)
    sends += scatter
    row = gram_chip[core, mine["y"], mine["x"]]
    for n, copy in enumerate(scatter):
        copy.wait_recv()
        row += gram_parts[n]
    gram_z[mine["z"]] = row
    spread = []
    for dz in range(1, NZ):
        slot = 16 + dz
        z = along("z", dz)
        copy = remote(
            gram_z.at[mine["z"]], gram_z.at[mine["z"]], gx_send.at[slot], gx_recv.at[slot], device(z=z))
        copy.start()
        sends.append(copy)
    for dz in range(1, NZ):
        slot = 16 + dz
        z = along("z", -dz)
        remote(gram_z.at[z], gram_z.at[z], gx_send.at[slot], gx_recv.at[slot], sibling).wait_recv()
    row = gram_z[0]
    for n in range(1, NZ):
        row += gram_z[n]
    gram_row[core, mine["y"], mine["x"]] = row
    for n, (dy, dx) in enumerate(plane):
        slot = 24 + n
        here = gram_row.at[core, mine["y"], mine["x"]]
        copy = remote(
            here, here, gx_send.at[slot], gx_recv.at[slot], device(y=along("y", dy), x=along("x", dx)))
        copy.start()
        sends.append(copy)
    for n, (dy, dx) in enumerate(plane):
        slot = 24 + n
        there = gram_row.at[core, along("y", -dy), along("x", -dx)]
        remote(there, there, gx_send.at[slot], gx_recv.at[slot], sibling).wait_recv()
    copy = remote(gram_row.at[core], gram_row.at[core], gx_send.at[40], gx_recv.at[40], sibling)
    copy.start()
    sends.append(copy)
    arriving = gram_row.at[1 - core]
    remote(arriving, arriving, gx_send.at[40], gx_recv.at[40], sibling).wait_recv()
    g_ref[...] = gram_row[...].reshape(256, 256)
    for copy in sends:
        copy.wait_send()


def exchange(velocity, basis_in):
    rows, snaps = velocity.shape
    rank = basis_in.shape[1]
    f32, bf16 = jnp.float32, jnp.bfloat16
    dma = pltpu.SemaphoreType.DMA
    return pl.pallas_call(
        exchange_kernel,
        out_shape=(
            jax.ShapeDtypeStruct((rows, rank), f32),
            jax.ShapeDtypeStruct((rank, rank), f32),
        ),
        in_specs=[pl.BlockSpec(memory_space=pl.ANY)] * 2,
        out_specs=[pl.BlockSpec(memory_space=pltpu.VMEM)] * 2,
        scratch_shapes=[
            pltpu.VMEM((rows, snaps), bf16),
            pltpu.VMEM((rows, snaps // 2), bf16),
            pltpu.VMEM((rows, rank), bf16),
            pltpu.VMEM((rows, rank), bf16),
            pltpu.VMEM((NX, NZ, NY, 64, 128), f32),
            pltpu.VMEM((2, NX, NZ, NY, 64, 128), bf16),
            pltpu.VMEM((2, rank, rank), f32),
            pltpu.VMEM((2, NY, NX, 8, rank), f32),
            pltpu.VMEM((NY * NX - 1, 8, rank), f32),
            pltpu.VMEM((NZ, 8, rank), f32),
            pltpu.VMEM((2, NY, NX, 8, rank), f32),
            *[pltpu.VMEM(shape, f32) for _, shape in RS_MESSAGES],
            dma((2 * NX + 1,)),
            dma((NX + 1,)),
            dma((NX + 1,)),
            dma((N_RS,)),
            dma((N_RS,)),
            dma((N_AG,)),
            dma((N_AG,)),
            dma((N_SIB,)),
            dma((N_SIB,)),
            dma((41,)),
            dma((41,)),
        ],
        compiler_params=pltpu.CompilerParams(
            collective_id=0, has_side_effects=True, vmem_limit_bytes=56 * 2**20
        ),
        cost_estimate=pl.CostEstimate(
            flops=4 * rows * snaps * rank, bytes_accessed=2 * rows * snaps, transcendentals=0
        ),
    )(velocity, basis_in)


def factor_kernel(scale, p_ref, g_ref, out_ref, r_ref, w, state):
    size = g_ref.shape[0]
    row = lax.broadcasted_iota(jnp.int32, (size, size), 0)
    col = lax.broadcasted_iota(jnp.int32, (size, size), 1)
    eye = (row == col).astype(jnp.float32)
    weight = jnp.where(row < col, 1.0, 0.5 * eye)
    gram = g_ref[...]
    diagonal = gram * eye
    unit_row = lax.rsqrt(jnp.sum(diagonal, axis=0, keepdims=True))
    unit_col = lax.rsqrt(jnp.sum(diagonal, axis=1, keepdims=True))
    scaled = gram * unit_row * unit_col

    w[...] = eye
    state[...] = scaled - eye

    def go_on(carry):
        count, norm = carry
        return (norm > 1e-6) & (norm < 1e4) & (count < 12)

    def improve():
        upper = state[...] * weight
        once = dot(w[...], upper, (1, 0), HIGHEST)
        w[...] = w[...] - once + dot(once, upper, (1, 0), HIGHEST)

    def step(carry):
        count, _ = carry
        improve()
        excess = dot(w[...], dot(scaled, w[...], (1, 0), HIGHEST), (0, 0), HIGHEST) - eye
        state[...] = excess
        return count + 1, jnp.sum(excess * excess)

    start = state[...]
    _, norm = lax.while_loop(go_on, step, (0, jnp.sum(start * start)))
    converged = norm <= 1e-6

    @pl.when(converged)
    def _():
        improve()

    @pl.when(jnp.logical_not(converged))
    def _():
        state[...] = scaled
        r_ref[...] = jnp.zeros_like(r_ref)
        lane = lax.broadcasted_iota(jnp.int32, (1, size), 1)

        def eliminate(j, _):
            pivot_row = jnp.where(lane >= j, state[pl.ds(j, 1), :], 0.0)
            pivot = jnp.sum(jnp.where(lane == j, pivot_row, 0.0), axis=1, keepdims=True)
            pivot_row = pivot_row / jnp.sqrt(pivot)
            r_ref[pl.ds(j, 1), :] = pivot_row
            pivot_col = jnp.sum(jnp.broadcast_to(pivot_row, (size, size)) * eye, axis=1, keepdims=True)
            state[...] = state[...] - pivot_col * pivot_row
            return 0

        lax.fori_loop(0, size, eliminate, 0)
        w[...] = jnp.zeros_like(w)

        def substitute(n, _):
            j = size - 1 - n
            line = r_ref[pl.ds(j, 1), :]
            pivot = jnp.sum(jnp.where(lane == j, line, 0.0), axis=1, keepdims=True)
            beyond = jnp.where(lane > j, line, 0.0)
            unit = jnp.where(lane == j, 1.0, 0.0)
            w[pl.ds(j, 1), :] = (unit - dot(beyond, w[...], (1, 0), HIGHEST)) / pivot
            return 0

        lax.fori_loop(0, size, substitute, 0)

    triangle = jnp.where(row <= col, dot(w[...], scaled, (0, 0), HIGHEST), 0.0)
    r_ref[...] = triangle / unit_row / scale
    out_ref[...] = dot(p_ref[...], w[...] * unit_col * scale, (1, 0), HIGHEST)


def factor(projected, gram, scale):
    rank = gram.shape[0]
    return pl.pallas_call(
        functools.partial(factor_kernel, scale),
        out_shape=(
            jax.ShapeDtypeStruct(projected.shape, jnp.float32),
            jax.ShapeDtypeStruct((rank, rank), jnp.float32),
        ),
        scratch_shapes=[pltpu.VMEM((rank, rank), jnp.float32)] * 2,
        compiler_params=pltpu.CompilerParams(vmem_limit_bytes=32 * 2**20),
    )(projected, gram)


def local(velocity, basis_in):
    projected, gram = exchange(velocity, basis_in)
    scale = float(lax.axis_size("rows") * velocity.shape[0]) ** 0.5
    return factor(projected, gram, scale)


def solution(mesh):
    in_specs = (P("rows", None), P("rows", None))
    out_specs = (P("rows", None), P())
    return jax.shard_map(local, mesh=mesh, in_specs=in_specs, out_specs=out_specs, check_vma=False)
```

time: 925 us -> 131 us (0.14)
  other arithmetic: 510 us -> 0 us
  blocking collectives: 148 us -> 0 us
  Pallas kernels: 0 us -> 128 us
  local copies, waits for them, and re-layouts: 107 us -> 1.98 us
  matrix products: 63.9 us -> 0 us
  waiting for transfers between devices: 62.3 us -> 0 us
  between operations: 14.1 us -> 0.65 us
  starting transfers between devices: 10.2 us -> 0 us
    another operation x82 -> x0, other arithmetic: 508 us -> none  [the longest x62 311 us: triangle(): return jnp.linalg.cholesky(gram_matrix).T]
    psum x1 -> x0, blocking collectives: 148 us -> none  [local(): coefficients = lax.psum(partial_sum, 'rows').astype(jnp.bfloat16)]
    pallas_call x0 -> x2, Pallas kernels: none -> 128 us  [the longest x1 118 us: exchange(): pl.pallas_call(exchange_kernel, out_shape=(jax.ShapeDtypeStruct((rows, ra...]
    gather x27 -> x0, local copies, waits for them, and re-layouts: 63.3 us -> none  [upper_half(): return jnp.triu(matrix, 1) + jnp.diag(0.5 * jnp.diagonal(matrix))]
    ppermute x8 -> x0, waiting for transfers between devices: 62.3 us -> none  [from_partner(): return lax.ppermute(value, axis, pairs)]
    dot_general x47 -> x0, matrix products: 45.6 us -> none  [the longest x18 14.6 us: gram_of(): lax.dot_general(matrix, matrix, (((0,), (0,)), ((), ())), precision=lax.P...]
    another operation x93 -> x0, local copies, waits for them, and re-layouts: 40.6 us -> none  [the longest x75 40.4 us: right_divide(): return jax.scipy.linalg.solve_triangular(r_factor.T, matrix.T, lower=True).T]
    another operation x48 -> x0, matrix products: 18.3 us -> none  [the longest x30 14 us: right_divide(): return jax.scipy.linalg.solve_triangular(r_factor.T, matrix.T, lower=True).T]
  transfers between devices with their start and end apart: 8 -> 0, of which waited for: 8 -> 0; matrix products, arithmetic and copies ran while one was open for 0% -> 0% of each run, Pallas kernels for 0% -> 0%
where the time goes in v1:
time: 131 us; the launch traced here: 130 us
  Pallas kernels  128 us (98%)
  local copies, waits for them, and re-layouts  1.98 us (2%)
    pallas_call x1, Pallas kernels, exchange(): pl.pallas_call(exchange_kernel, out_shape=(jax.ShapeDtypeStruct((rows, ra...  118 us
    pallas_call x1, Pallas kernels, factor(): pl.pallas_call(functools.partial(factor_kernel, scale), out_shape=(jax.Sh...  9.61 us

profile of v1, /device:TPU:1, one launch (start us, length us, event | category | flops | bytes accessed | tf_op | source)
XLA Modules:
  0.0 130.4 jit_solution(2805783335473909542)
XLA Ops:
  0.6 118.2 %shard_map.41 = (f32[512,256]{1,0:T(8,128)}, f32[256,256]{1,0:T(8,128)}) custom-call(bf16[512,8192]{1,0:T(8,128)(2,1)} %refs_0_.1, bf16[512,256]{1,0:T(8,128)(2,1)} %refs_1_.1), custom_call_target="tpu_custom_call" | custom-call | flops 4294967296 | bytes 8388608 | tf_op jit(solution)/shard_map/pallas_call | solution.py:361
  118.8 0.0 copy-start
  118.8 1.0 copy-done
  119.8 0.0 copy-start.1
  119.8 0.9 copy-done.1
  120.8 9.6 %shard_map.42 = (f32[512,256]{1,0:T(8,128)}, f32[256,256]{1,0:T(8,128)}) custom-call(f32[512,256]{1,0:T(8,128)S(1)} %copy-done, f32[256,256]{1,0:T(8,128)S(1)} %copy-done.1), custom_call_target="tpu_custom_call" | custom-call | tf_op jit(solution)/shard_map/pallas_call | solution.py:478
Async XLA Ops:
  118.8 1.0 copy-start
  119.8 0.9 copy-start.1

commit v2 on v1

v2 whole, which is shorter than its diff:
```python
import functools

import jax
import jax.numpy as jnp
from jax import lax
from jax.experimental import pallas as pl
from jax.experimental.pallas import tpu as pltpu
from jax.sharding import PartitionSpec as P

NY, NX, NZ = 4, 4, 8
SIZE = {"x": NX, "z": NZ, "y": NY}
MESH = pl.DeviceIdType.MESH
HIGHEST = lax.Precision.HIGHEST


PARTS = (("x", "y"), ("y", "x"))
PIECE = 32
FAR_FIRST = (2, 1, 3)
SCALE = 2.0**17


def dot(a, b, contract, precision=None):
    return lax.dot_general(
        a, b, ((contract[:1], contract[1:]), ((), ())),
        precision=precision, preferred_element_type=jnp.float32,
    )


def encode(value):
    scaled = value * SCALE
    return (scaled * scaled * (scaled * jnp.abs(scaled))).astype(jnp.bfloat16)


def decode(code):
    wide = code.astype(jnp.float32)
    power = jnp.maximum(jnp.abs(wide), 1e-37)
    root = lax.rsqrt(power)
    return wide * root * (lax.rsqrt(power * root) * (1.0 / SCALE))


def exchange_kernel(
    v_hbm, b_hbm, p_ref, g_ref,
    v, v_sib, b, b_sib, total, coded, in_first, in_second, in_z, gathered,
    gram_in, gram_chip, gram_parts, gram_z, gram_row,
    load_sem, sib_send, sib_recv, first_send, first_recv, second_send, second_recv,
    z_send, z_recv, out_z_send, out_z_recv, out_second_send, out_second_recv,
    out_first_send, out_first_recv, fwd_send, fwd_recv, gx_send, gx_recv,
):
    me = lax.axis_index("rows")
    core = me % 2
    mine = {"z": me // 2 % NZ, "x": me // (2 * NZ) % NX, "y": me // (2 * NZ * NX)}

    def device(**moved):
        at = {**mine, "core": core, **moved}
        return (((at["y"] * NX + at["x"]) * NZ + at["z"]) * 2 + at["core"],)

    def along(axis, offset):
        return (mine[axis] + offset + SIZE[axis]) % SIZE[axis]

    sibling = device(core=1 - core)

    def remote(source, target, send, recv, to):
        return pltpu.make_async_remote_copy(
            src_ref=source, dst_ref=target, send_sem=send, recv_sem=recv,
            device_id=to, device_id_type=MESH,
        )

    sends = []

    def start(copy):
        copy.start()
        sends.append(copy)

    half = v_sib.shape[1]
    wide = half // NX

    def columns(which_core, k):
        return pl.ds(pl.multiple_of(which_core * half + k * wide, 128), wide)

    order = [along("x", offset) for offset in FAR_FIRST + (0,)]
    loads = []
    for n, (which, k) in enumerate([(core, k) for k in order] + [(1 - core, k) for k in range(NX)]):
        loads.append(pltpu.make_async_copy(
            v_hbm.at[:, columns(which, k)], v.at[:, columns(which, k)], load_sem.at[n]))
    load_b = pltpu.make_async_copy(b_hbm, b, load_sem.at[2 * NX])
    load_b.start()
    for load in loads:
        load.start()

    partners = [sibling]
    for dy in range(NY):
        for dx in range(NX):
            if dy or dx:
                partners.append(device(y=along("y", dy), x=along("x", dx)))
    for dz in range(1, NZ):
        partners.append(device(z=along("z", dz)))
    barrier = pltpu.get_barrier_semaphore()
    for partner in partners:
        pl.semaphore_signal(barrier, inc=1, device_id=partner, device_id_type=MESH)
    pl.semaphore_wait(barrier, len(partners))

    copy_b = remote(b_hbm, b_sib, sib_send.at[NX], sib_recv.at[NX], sibling)
    start(copy_b)
    copies_v = []
    for n, k in enumerate(order):
        copy = remote(
            v_hbm.at[:, columns(1 - core, k)], v_sib.at[:, pl.ds(n * wide, wide)],
            sib_send.at[n], sib_recv.at[n], sibling)
        start(copy)
        copies_v.append(copy)

    load_b.wait()
    b_t = b[...].T
    copy_b.wait_recv()
    b_sib_t = b_sib[...].T

    def first_copy(part, away, o2):
        first, _ = PARTS[part]
        k = along(first, away)
        slot = (away - 1) * 4 + o2
        return remote(
            coded.at[part, k, o2], in_first.at[part, away - 1, o2],
            first_send.at[part, slot], first_recv.at[part, slot], device(**{first: k}))

    for n, k in enumerate(order):
        loads[n].wait()
        copies_v[n].wait_recv()
        product = dot(b_t, v[:, columns(core, k)], (1, 0))
        product += dot(b_sib_t, v_sib[:, n * wide:(n + 1) * wide], (1, 0))
        for part in range(2):
            for o2 in range(4):
                ranks = slice(part * 128 + o2 * PIECE, part * 128 + (o2 + 1) * PIECE)
                for z in range(NZ):
                    tile = product[ranks, z * 128:(z + 1) * 128]
                    total[part, k, o2, z] = tile
                    coded[part, k, o2, z] = encode(tile)
        for j2 in FAR_FIRST + (0,):
            if n < 3:
                first_copy(0, FAR_FIRST[n], along("y", j2)).start()
        away = (k - mine["y"] + NY) % NY

        @pl.when(away != 0)
        def _():
            for j2 in FAR_FIRST + (0,):
                first_copy(1, away, along("x", j2)).start()

    sums = [None, None]
    for j2 in FAR_FIRST + (0,):
        for part, (first, second) in enumerate(PARTS):
            o2 = along(second, j2)
            block = total[part, mine[first], o2]
            for away in (2, 1, 3):
                first_copy(part, away, o2).wait_recv()
                block += decode(in_first[part, away - 1, o2])
            if j2:
                coded[part, mine[first], o2] = encode(block)
                start(remote(
                    coded.at[part, mine[first], o2], in_second.at[part, j2 - 1],
                    second_send.at[part, j2 - 1], second_recv.at[part, j2 - 1], device(**{second: o2})))
            else:
                total[part, mine[first], o2] = block

    for part, (first, second) in enumerate(PARTS):
        block = total[part, mine[first], mine[second]]
        for j2 in FAR_FIRST:
            slot = in_second.at[part, j2 - 1]
            remote(slot, slot, second_send.at[part, j2 - 1], second_recv.at[part, j2 - 1], sibling).wait_recv()
            block += decode(in_second[part, j2 - 1])
        total[part, mine[first], mine[second]] = block
        coded[part, mine[first], mine[second]] = encode(block)
        for dz in (4, 3, 5, 2, 6, 1, 7):
            z = along("z", dz)
            start(remote(
                coded.at[part, mine[first], mine[second], z], in_z.at[part, dz - 1],
                z_send.at[part, dz - 1], z_recv.at[part, dz - 1], device(z=z)))

    for part, (first, second) in enumerate(PARTS):
        piece = total[part, mine[first], mine[second], mine["z"]]
        for dz in (1, 7, 2, 6, 3, 5, 4):
            slot = in_z.at[part, dz - 1]
            remote(slot, slot, z_send.at[part, dz - 1], z_recv.at[part, dz - 1], sibling).wait_recv()
            piece += decode(in_z[part, dz - 1])
        here = gathered.at[core, part, mine[first], mine[second], mine["z"]]
        here[...] = piece.astype(jnp.bfloat16)
        for dz in (4, 3, 5, 2, 6, 1, 7):
            start(remote(
                here, here, out_z_send.at[part, dz - 1], out_z_recv.at[part, dz - 1],
                device(z=along("z", dz))))

    def spread(part, j2):
        first, second = PARTS[part]
        block = gathered.at[core, part, mine[first], along(second, -j2)]
        for away in FAR_FIRST:
            slot = (away - 1) * 4 + j2
            start(remote(
                block, block, out_first_send.at[part, slot], out_first_recv.at[part, slot],
                device(**{first: along(first, away)})))
        start(remote(block, block, fwd_send.at[part, j2], fwd_recv.at[part, j2], sibling))

    for part, (first, second) in enumerate(PARTS):
        for dz in (1, 7, 2, 6, 3, 5, 4):
            there = gathered.at[core, part, mine[first], mine[second], along("z", -dz)]
            remote(there, there, out_z_send.at[part, dz - 1], out_z_recv.at[part, dz - 1], sibling).wait_recv()
        block = gathered.at[core, part, mine[first], mine[second]]
        for j2 in FAR_FIRST:
            start(remote(
                block, block, out_second_send.at[part, j2 - 1], out_second_recv.at[part, j2 - 1],
                device(**{second: along(second, j2)})))
        spread(part, 0)
    for j2 in (1, 3, 2):
        for part, (first, second) in enumerate(PARTS):
            there = gathered.at[core, part, mine[first], along(second, -j2)]
            remote(
                there, there, out_second_send.at[part, j2 - 1], out_second_recv.at[part, j2 - 1], sibling
            ).wait_recv()
            spread(part, j2)

    for load in loads[NX:]:
        load.wait()
    projected = [None, None]

    def add_chunk(which, part, k):
        ranks = jnp.concatenate(
            [gathered[which, part, k, :, z].reshape(128, 128) for z in range(NZ)], axis=1)
        term = dot(v[:, columns(which, k)], ranks, (1, 1))
        projected[part] = term if projected[part] is None else projected[part] + term

    def from_sibling(part, away):
        first, second = PARTS[part]
        k = along(first, -away)
        for j2 in range(4):
            there = gathered.at[1 - core, part, k, along(second, -j2)]
            slot = away * 4 + j2
            remote(there, there, fwd_send.at[part, slot], fwd_recv.at[part, slot], sibling).wait_recv()
        add_chunk(1 - core, part, k)

    for part, (first, second) in enumerate(PARTS):
        add_chunk(core, part, mine[first])
    for away, done in ((1, 0), (3, 1), (2, 3)):
        for part, (first, second) in enumerate(PARTS):
            k = along(first, -away)
            for j2 in (0, 1, 3, 2):
                there = gathered.at[core, part, k, along(second, -j2)]
                slot = (away - 1) * 4 + j2
                remote(
                    there, there, out_first_send.at[part, slot], out_first_recv.at[part, slot], sibling
                ).wait_recv()
                slot = away * 4 + j2
                start(remote(there, there, fwd_send.at[part, slot], fwd_recv.at[part, slot], sibling))
            add_chunk(core, part, k)
        for part in range(2):
            from_sibling(part, done)
    for part in range(2):
        from_sibling(part, 2)

    projected = jnp.concatenate(projected, axis=1)
    p_ref[...] = projected
    gram_in[0] = dot(projected, projected, (0, 0), HIGHEST)

    copy = remote(gram_in.at[0], gram_in.at[1], gx_send.at[0], gx_recv.at[0], sibling)
    start(copy)
    copy.wait_recv()
    gram_chip[...] = (gram_in[0] + gram_in[1]).reshape(2, NY, NX, 8, 256)

    plane = [(dy, dx) for dy in range(NY) for dx in range(NX) if dy or dx]
    scatter = []
    for n, (dy, dx) in enumerate(plane):
        y, x = along("y", dy), along("x", dx)
        copy = remote(
            gram_chip.at[core, y, x], gram_parts.at[n], gx_send.at[1 + n], gx_recv.at[1 + n], device(y=y, x=x))
        copy.start()
        scatter.append(copy)
    sends += scatter
    row = gram_chip[core, mine["y"], mine["x"]]
    for n, copy in enumerate(scatter):
        copy.wait_recv()
        row += gram_parts[n]
    gram_z[mine["z"]] = row
    spread = []
    for dz in range(1, NZ):
        slot = 16 + dz
        z = along("z", dz)
        copy = remote(
            gram_z.at[mine["z"]], gram_z.at[mine["z"]], gx_send.at[slot], gx_recv.at[slot], device(z=z))
        start(copy)
    for dz in range(1, NZ):
        slot = 16 + dz
        z = along("z", -dz)
        remote(gram_z.at[z], gram_z.at[z], gx_send.at[slot], gx_recv.at[slot], sibling).wait_recv()
    row = gram_z[0]
    for n in range(1, NZ):
        row += gram_z[n]
    gram_row[core, mine["y"], mine["x"]] = row
    for n, (dy, dx) in enumerate(plane):
        slot = 24 + n
        here = gram_row.at[core, mine["y"], mine["x"]]
        copy = remote(
            here, here, gx_send.at[slot], gx_recv.at[slot], device(y=along("y", dy), x=along("x", dx)))
        start(copy)
    for n, (dy, dx) in enumerate(plane):
        slot = 24 + n
        there = gram_row.at[core, along("y", -dy), along("x", -dx)]
        remote(there, there, gx_send.at[slot], gx_recv.at[slot], sibling).wait_recv()
    copy = remote(gram_row.at[core], gram_row.at[core], gx_send.at[40], gx_recv.at[40], sibling)
    start(copy)
    arriving = gram_row.at[1 - core]
    remote(arriving, arriving, gx_send.at[40], gx_recv.at[40], sibling).wait_recv()
    g_ref[...] = gram_row[...].reshape(256, 256)
    for part, (first, second) in enumerate(PARTS):
        for away in FAR_FIRST:
            for j2 in range(4):
                first_copy(part, away, along(second, j2)).wait_send()
    for copy in sends:
        copy.wait_send()


def exchange(velocity, basis_in):
    rows, snaps = velocity.shape
    rank = basis_in.shape[1]
    f32, bf16 = jnp.float32, jnp.bfloat16

    def pair(*shape):
        return [pltpu.SemaphoreType.DMA(shape)] * 2

    return pl.pallas_call(
        exchange_kernel,
        out_shape=(
            jax.ShapeDtypeStruct((rows, rank), f32),
            jax.ShapeDtypeStruct((rank, rank), f32),
        ),
        in_specs=[pl.BlockSpec(memory_space=pl.ANY)] * 2,
        out_specs=[pl.BlockSpec(memory_space=pltpu.VMEM)] * 2,
        scratch_shapes=[
            pltpu.VMEM((rows, snaps), bf16),
            pltpu.VMEM((rows, snaps // 2), bf16),
            pltpu.VMEM((rows, rank), bf16),
            pltpu.VMEM((rows, rank), bf16),
            pltpu.VMEM((2, 4, 4, NZ, PIECE, 128), f32),
            pltpu.VMEM((2, 4, 4, NZ, PIECE, 128), bf16),
            pltpu.VMEM((2, 3, 4, NZ, PIECE, 128), bf16),
            pltpu.VMEM((2, 3, NZ, PIECE, 128), bf16),
            pltpu.VMEM((2, NZ - 1, PIECE, 128), bf16),
            pltpu.VMEM((2, 2, 4, 4, NZ, PIECE, 128), bf16),
            pltpu.VMEM((2, rank, rank), f32),
            pltpu.VMEM((2, NY, NX, 8, rank), f32),
            pltpu.VMEM((NY * NX - 1, 8, rank), f32),
            pltpu.VMEM((NZ, 8, rank), f32),
            pltpu.VMEM((2, NY, NX, 8, rank), f32),
            pltpu.SemaphoreType.DMA((2 * NX + 1,)),
            *pair(NX + 1),
            *pair(2, 12),
            *pair(2, 3),
            *pair(2, NZ - 1),
            *pair(2, NZ - 1),
            *pair(2, 3),
            *pair(2, 12),
            *pair(2, 16),
            *pair(41),
        ],
        compiler_params=pltpu.CompilerParams(
            collective_id=0, has_side_effects=True, vmem_limit_bytes=48 * 2**20
        ),
        cost_estimate=pl.CostEstimate(
            flops=4 * rows * snaps * rank, bytes_accessed=2 * rows * snaps, transcendentals=0
        ),
    )(velocity, basis_in)


def factor_kernel(scale, p_ref, g_ref, out_ref, r_ref, w, state):
    size = g_ref.shape[0]
    row = lax.broadcasted_iota(jnp.int32, (size, size), 0)
    col = lax.broadcasted_iota(jnp.int32, (size, size), 1)
    eye = (row == col).astype(jnp.float32)
    weight = jnp.where(row < col, 1.0, 0.5 * eye)
    gram = g_ref[...]
    diagonal = gram * eye
    unit_row = lax.rsqrt(jnp.sum(diagonal, axis=0, keepdims=True))
    unit_col = lax.rsqrt(jnp.sum(diagonal, axis=1, keepdims=True))
    scaled = gram * unit_row * unit_col

    w[...] = eye
    state[...] = scaled - eye

    def go_on(carry):
        count, norm = carry
        return (norm > 1e-6) & (norm < 1e4) & (count < 12)

    def improve():
        upper = state[...] * weight
        once = dot(w[...], upper, (1, 0), HIGHEST)
        w[...] = w[...] - once + dot(once, upper, (1, 0), HIGHEST)

    def step(carry):
        count, _ = carry
        improve()
        excess = dot(w[...], dot(scaled, w[...], (1, 0), HIGHEST), (0, 0), HIGHEST) - eye
        state[...] = excess
        return count + 1, jnp.sum(excess * excess)

    start = state[...]
    _, norm = lax.while_loop(go_on, step, (0, jnp.sum(start * start)))
    converged = norm <= 1e-6

    @pl.when(converged)
    def _():
        improve()

    @pl.when(jnp.logical_not(converged))
    def _():
        state[...] = scaled
        r_ref[...] = jnp.zeros_like(r_ref)
        lane = lax.broadcasted_iota(jnp.int32, (1, size), 1)

        def eliminate(j, _):
            pivot_row = jnp.where(lane >= j, state[pl.ds(j, 1), :], 0.0)
            pivot = jnp.sum(jnp.where(lane == j, pivot_row, 0.0), axis=1, keepdims=True)
            pivot_row = pivot_row / jnp.sqrt(pivot)
            r_ref[pl.ds(j, 1), :] = pivot_row
            pivot_col = jnp.sum(jnp.broadcast_to(pivot_row, (size, size)) * eye, axis=1, keepdims=True)
            state[...] = state[...] - pivot_col * pivot_row
            return 0

        lax.fori_loop(0, size, eliminate, 0)
        w[...] = jnp.zeros_like(w)

        def substitute(n, _):
            j = size - 1 - n
            line = r_ref[pl.ds(j, 1), :]
            pivot = jnp.sum(jnp.where(lane == j, line, 0.0), axis=1, keepdims=True)
            beyond = jnp.where(lane > j, line, 0.0)
            unit = jnp.where(lane == j, 1.0, 0.0)
            w[pl.ds(j, 1), :] = (unit - dot(beyond, w[...], (1, 0), HIGHEST)) / pivot
            return 0

        lax.fori_loop(0, size, substitute, 0)

    triangle = jnp.where(row <= col, dot(w[...], scaled, (0, 0), HIGHEST), 0.0)
    r_ref[...] = triangle / unit_row / scale
    out_ref[...] = dot(p_ref[...], w[...] * unit_col * scale, (1, 0), HIGHEST)


def factor(projected, gram, scale):
    rank = gram.shape[0]
    return pl.pallas_call(
        functools.partial(factor_kernel, scale),
        out_shape=(
            jax.ShapeDtypeStruct(projected.shape, jnp.float32),
            jax.ShapeDtypeStruct((rank, rank), jnp.float32),
        ),
        scratch_shapes=[pltpu.VMEM((rank, rank), jnp.float32)] * 2,
        compiler_params=pltpu.CompilerParams(vmem_limit_bytes=32 * 2**20),
    )(projected, gram)


def local(velocity, basis_in):
    projected, gram = exchange(velocity, basis_in)
    scale = float(lax.axis_size("rows") * velocity.shape[0]) ** 0.5
    return factor(projected, gram, scale)


def solution(mesh):
    in_specs = (P("rows", None), P("rows", None))
    out_specs = (P("rows", None), P())
    return jax.shard_map(local, mesh=mesh, in_specs=in_specs, out_specs=out_specs, check_vma=False)
```

time: 131 us -> 102 us (0.78)
  Pallas kernels: 128 us -> 100 us
    pallas_call x1, Pallas kernels: 118 us -> 90.5 us  [exchange(): pl.pallas_call(exchange_kernel, out_shape=(jax.ShapeDtypeStruct((rows, ra...]
where the time goes in v2:
time: 102 us
  Pallas kernels  100 us (98%)
    pallas_call x1, Pallas kernels, exchange(): pl.pallas_call(exchange_kernel, out_shape=(jax.ShapeDtypeStruct((rows, ra...  90.5 us
    pallas_call x1, Pallas kernels, factor(): pl.pallas_call(functools.partial(factor_kernel, scale), out_shape=(jax.Sh...  9.79 us

profile of v2, /device:TPU:1, one launch (start us, length us, event | category | flops | bytes accessed | tf_op | source)
XLA Modules:
  0.0 101.9 jit_solution(1056392687991255055)
XLA Ops:
  0.6 0.0 copy-start
  0.6 0.9 copy-done
  1.6 90.5 %shard_map.41 = (f32[512,256]{1,0:T(8,128)S(1)}, f32[256,256]{1,0:T(8,128)S(1)}) custom-call(bf16[512,8192]{1,0:T(8,128)(2,1)} %v_hbm.1, bf16[512,256]{1,0:T(8,128)(2,1)S(1)} %copy-done), custom_call_target="tpu_custom_call" | custom-call | flops 4294967296 | bytes 8388608 | tf_op jit(solution)/shard_map/pallas_call | solution.py:325
  92.1 9.8 %shard_map.42 = (f32[512,256]{1,0:T(8,128)}, f32[256,256]{1,0:T(8,128)}) custom-call(f32[512,256]{1,0:T(8,128)S(1)} %get-tuple-element.4.p_ref, f32[256,256]{1,0:T(8,128)S(1)} %get-tuple-element.5.g_ref), custom_call_target="tpu_custom_call" | custom-call | tf_op jit(solution)/shard_map/pallas_call | solution.py:444
Async XLA Ops:
  0.6 1.0 copy-start

commit v3 on v2

v3 whole, which is shorter than its diff:
```python
import functools

import jax
import jax.numpy as jnp
from jax import lax
from jax.experimental import pallas as pl
from jax.experimental.pallas import tpu as pltpu
from jax.sharding import PartitionSpec as P

NY, NX, NZ = 4, 4, 8
SIZE = {"x": NX, "z": NZ, "y": NY}
MESH = pl.DeviceIdType.MESH
HIGHEST = lax.Precision.HIGHEST


PARTS = (("x", "y"), ("y", "x"))
PIECE = 16
BLOCKS = 4
FAR_FIRST = (2, 1, 3)
NEAR_FIRST = (1, 3, 2)
Z_FAR_FIRST = (4, 3, 5, 2, 6, 1, 7)
Z_NEAR_FIRST = Z_FAR_FIRST[::-1]
SCALE = 2.0**17


def dot(a, b, contract, precision=None):
    return lax.dot_general(
        a, b, ((contract[:1], contract[1:]), ((), ())),
        precision=precision, preferred_element_type=jnp.float32,
    )


def encode(value):
    scaled = value * SCALE
    return (scaled * scaled * (scaled * jnp.abs(scaled))).astype(jnp.bfloat16)


def decode(code):
    wide = code.astype(jnp.float32)
    power = jnp.maximum(jnp.abs(wide), 1e-37)
    root = lax.rsqrt(power)
    return wide * root * (lax.rsqrt(power * root) * (1.0 / SCALE))


def exchange_kernel(
    v_hbm, b_hbm, p_ref, g_ref,
    v, v_sib, b, b_sib, total, coded, in_first, in_second, in_z, gathered,
    gram_in, gram_chip, gram_parts, gram_z, gram_row,
    load_sem, sib_send, sib_recv, first_send, first_recv, second_send, second_recv,
    z_send, z_recv, out_z_send, out_z_recv, out_second_send, out_second_recv,
    out_first_send, out_first_recv, fwd_send, fwd_recv, gx_send, gx_recv,
):
    me = lax.axis_index("rows")
    core = me % 2
    mine = {"z": me // 2 % NZ, "x": me // (2 * NZ) % NX, "y": me // (2 * NZ * NX)}

    def device(**moved):
        at = {**mine, "core": core, **moved}
        return (((at["y"] * NX + at["x"]) * NZ + at["z"]) * 2 + at["core"],)

    def along(axis, offset):
        return (mine[axis] + offset + SIZE[axis]) % SIZE[axis]

    sibling = device(core=1 - core)

    def remote(source, target, send, recv, to):
        return pltpu.make_async_remote_copy(
            src_ref=source, dst_ref=target, send_sem=send, recv_sem=recv,
            device_id=to, device_id_type=MESH,
        )

    sends = []

    def start(copy):
        copy.start()
        sends.append(copy)

    half = v_sib.shape[1]
    wide = half // (2 * NX)

    def columns(which_core, group, k):
        return pl.ds(pl.multiple_of(which_core * half + (2 * k + group) * wide, 128), wide)

    order = [(group, along("x", offset)) for group in range(2) for offset in FAR_FIRST + (0,)]
    loads = []
    for group, k in order:
        loads.append(pltpu.make_async_copy(
            v_hbm.at[:, columns(core, group, k)], v.at[:, columns(core, group, k)], load_sem.at[len(loads)]))
    others = pl.ds(pl.multiple_of((1 - core) * half, 128), half)
    loads.append(pltpu.make_async_copy(v_hbm.at[:, others], v.at[:, others], load_sem.at[len(loads)]))
    load_b = pltpu.make_async_copy(b_hbm, b, load_sem.at[len(loads)])
    load_b.start()
    for load in loads:
        load.start()

    partners = [sibling]
    for dy in range(NY):
        for dx in range(NX):
            if dy or dx:
                partners.append(device(y=along("y", dy), x=along("x", dx)))
    for dz in range(1, NZ):
        partners.append(device(z=along("z", dz)))
    barrier = pltpu.get_barrier_semaphore()
    for partner in partners:
        pl.semaphore_signal(barrier, inc=1, device_id=partner, device_id_type=MESH)
    pl.semaphore_wait(barrier, len(partners))

    copy_b = remote(b_hbm, b_sib, sib_send.at[8], sib_recv.at[8], sibling)
    start(copy_b)
    copies_v = []
    for n, (group, k) in enumerate(order):
        copy = remote(
            v_hbm.at[:, columns(1 - core, group, k)], v_sib.at[:, pl.ds(n * wide, wide)],
            sib_send.at[n], sib_recv.at[n], sibling)
        start(copy)
        copies_v.append(copy)

    load_b.wait()
    b_t = b[...].T
    copy_b.wait_recv()
    b_sib_t = b_sib[...].T

    def first_copy(group, part, away):
        first, _ = PARTS[part]
        k = along(first, away)
        return remote(
            coded.at[group, part, k], in_first.at[group, part, away - 1],
            first_send.at[group, part, away - 1], first_recv.at[group, part, away - 1], device(**{first: k}))

    for n, (group, k) in enumerate(order):
        loads[n].wait()
        copies_v[n].wait_recv()
        product = dot(b_t, v[:, columns(core, group, k)], (1, 0))
        product += dot(b_sib_t, v_sib[:, n * wide:(n + 1) * wide], (1, 0))
        for part in range(2):
            for z in range(NZ):
                for o2 in range(4):
                    rank = part * 128 + z % 2 * 64 + o2 * PIECE
                    tile = product[rank:rank + PIECE, z // 2 * 128:(z // 2 + 1) * 128]
                    total[group, part, k, o2, z] = tile
                    coded[group, part, k, o2, z] = encode(tile)
        if n % 4 < 3:
            first_copy(group, 0, FAR_FIRST[n % 4]).start()
        away = (k - mine["y"] + NY) % NY

        @pl.when(away != 0)
        def _():
            first_copy(group, 1, away).start()

    def sum_first(group):
        for part, (first, second) in enumerate(PARTS):
            for away in FAR_FIRST:
                first_copy(group, part, away).wait_recv()
            for j2 in FAR_FIRST + (0,):
                o2 = along(second, j2)
                block = total[group, part, mine[first], o2]
                for away in FAR_FIRST:
                    block += decode(in_first[group, part, away - 1, o2])
                if j2:
                    coded[group, part, mine[first], o2] = encode(block)
                    start(remote(
                        coded.at[group, part, mine[first], o2], in_second.at[group, part, j2 - 1],
                        second_send.at[group, part, j2 - 1], second_recv.at[group, part, j2 - 1],
                        device(**{second: o2})))
                else:
                    total[group, part, mine[first], o2] = block

    def sum_second(group):
        for part, (first, second) in enumerate(PARTS):
            at = (group, part, mine[first], mine[second])
            block = total[at]
            for j2 in FAR_FIRST:
                slot = in_second.at[group, part, j2 - 1]
                remote(
                    slot, slot, second_send.at[group, part, j2 - 1], second_recv.at[group, part, j2 - 1], sibling
                ).wait_recv()
                block += decode(in_second[group, part, j2 - 1])
            total[at] = block
            coded[at] = encode(block)
            for dz in Z_FAR_FIRST:
                z = along("z", dz)
                start(remote(
                    coded.at[at + (z,)], in_z.at[group, part, dz - 1],
                    z_send.at[group, part, dz - 1], z_recv.at[group, part, dz - 1], device(z=z)))

    def spread_z(group):
        for part, (first, second) in enumerate(PARTS):
            piece = total[group, part, mine[first], mine[second], mine["z"]]
            for dz in Z_NEAR_FIRST:
                slot = in_z.at[group, part, dz - 1]
                remote(
                    slot, slot, z_send.at[group, part, dz - 1], z_recv.at[group, part, dz - 1], sibling
                ).wait_recv()
                piece += decode(in_z[group, part, dz - 1])
            here = gathered.at[core, group, part, mine[first], mine[second], mine["z"]]
            here[...] = piece.astype(jnp.bfloat16)
            for dz in Z_FAR_FIRST:
                start(remote(
                    here, here, out_z_send.at[group, part, dz - 1], out_z_recv.at[group, part, dz - 1],
                    device(z=along("z", dz))))

    def spread_second(group):
        for part, (first, second) in enumerate(PARTS):
            for dz in Z_NEAR_FIRST:
                there = gathered.at[core, group, part, mine[first], mine[second], along("z", -dz)]
                remote(
                    there, there, out_z_send.at[group, part, dz - 1], out_z_recv.at[group, part, dz - 1], sibling
                ).wait_recv()
            block = gathered.at[core, group, part, mine[first], mine[second]]
            for j2 in FAR_FIRST:
                start(remote(
                    block, block, out_second_send.at[group, part, j2 - 1],
                    out_second_recv.at[group, part, j2 - 1], device(**{second: along(second, j2)})))

    def forward(group, part, away):
        block = gathered.at[core, group, part, along(PARTS[part][0], -away)]
        start(remote(
            block, block, fwd_send.at[group, part, away], fwd_recv.at[group, part, away], sibling))

    def spread_first(group):
        for part, (first, second) in enumerate(PARTS):
            for j2 in NEAR_FIRST:
                there = gathered.at[core, group, part, mine[first], along(second, -j2)]
                remote(
                    there, there, out_second_send.at[group, part, j2 - 1],
                    out_second_recv.at[group, part, j2 - 1], sibling
                ).wait_recv()
            block = gathered.at[core, group, part, mine[first]]
            for away in FAR_FIRST:
                start(remote(
                    block, block, out_first_send.at[group, part, away - 1],
                    out_first_recv.at[group, part, away - 1], device(**{first: along(first, away)})))
            forward(group, part, 0)

    def add_chunk(which, group, part, away):
        k = along(PARTS[part][0], -away)
        ranks = jnp.concatenate([
            jnp.concatenate([
                gathered[which, group, part, k, :, 2 * n + h].reshape(4 * PIECE, 128) for h in range(2)
            ], axis=0)
            for n in range(BLOCKS)
        ], axis=1)
        term = dot(v[:, columns(which, group, k)], ranks, (1, 1))
        p_ref[:, part * 128:(part + 1) * 128] += term

    def from_chip(group, away):
        for part, (first, second) in enumerate(PARTS):
            if away:
                there = gathered.at[core, group, part, along(first, -away)]
                remote(
                    there, there, out_first_send.at[group, part, away - 1],
                    out_first_recv.at[group, part, away - 1], sibling
                ).wait_recv()
                forward(group, part, away)
        for part in range(2):
            add_chunk(core, group, part, away)

    def from_sibling(group, away):
        for part, (first, second) in enumerate(PARTS):
            there = gathered.at[1 - core, group, part, along(first, -away)]
            remote(
                there, there, fwd_send.at[group, part, away], fwd_recv.at[group, part, away], sibling
            ).wait_recv()
            add_chunk(1 - core, group, part, away)

    sum_first(0)
    sum_second(0)
    sum_first(1)
    spread_z(0)
    sum_second(1)
    spread_second(0)
    spread_z(1)
    spread_first(0)
    p_ref[...] = jnp.zeros_like(p_ref)
    loads[8].wait()
    from_chip(0, 0)
    spread_second(1)
    from_chip(0, 1)
    from_sibling(0, 0)
    spread_first(1)
    from_chip(0, 3)
    from_chip(1, 0)
    from_sibling(0, 1)
    from_chip(0, 2)
    from_sibling(0, 3)
    from_sibling(1, 0)
    from_chip(1, 1)
    from_sibling(0, 2)
    from_chip(1, 3)
    from_sibling(1, 1)
    from_chip(1, 2)
    from_sibling(1, 3)
    from_sibling(1, 2)

    projected = p_ref[...]
    gram_in[0] = dot(projected, projected, (0, 0), HIGHEST)

    copy = remote(gram_in.at[0], gram_in.at[1], gx_send.at[0], gx_recv.at[0], sibling)
    start(copy)
    copy.wait_recv()
    gram_chip[...] = (gram_in[0] + gram_in[1]).reshape(NY, NX, 16, 256)

    plane = [(dy, dx) for dy in (2, 1, 3, 0) for dx in (2, 1, 3, 0) if dy or dx]
    scatter = []
    for n, (dy, dx) in enumerate(plane):
        y, x = along("y", dy), along("x", dx)
        copy = remote(
            gram_chip.at[y, x], gram_parts.at[n], gx_send.at[1 + n], gx_recv.at[1 + n], device(y=y, x=x))
        start(copy)
        scatter.append(copy)
    row = gram_chip[mine["y"], mine["x"]]
    for n, copy in reversed(list(enumerate(scatter))):
        copy.wait_recv()
        row += gram_parts[n]
    gram_z[mine["z"]] = row
    for dz in Z_FAR_FIRST:
        slot = 16 + dz
        here = gram_z.at[mine["z"]]
        start(remote(here, here, gx_send.at[slot], gx_recv.at[slot], device(z=along("z", dz))))
    for dz in Z_NEAR_FIRST:
        slot = 16 + dz
        there = gram_z.at[along("z", -dz)]
        remote(there, there, gx_send.at[slot], gx_recv.at[slot], sibling).wait_recv()
    row = gram_z[0]
    for n in range(1, NZ):
        row += gram_z[n]
    gram_row[mine["y"], mine["x"]] = row
    for n, (dy, dx) in enumerate(plane):
        slot = 24 + n
        here = gram_row.at[mine["y"], mine["x"]]
        start(remote(
            here, here, gx_send.at[slot], gx_recv.at[slot], device(y=along("y", dy), x=along("x", dx))))
    for n, (dy, dx) in enumerate(plane):
        slot = 24 + n
        there = gram_row.at[along("y", -dy), along("x", -dx)]
        remote(there, there, gx_send.at[slot], gx_recv.at[slot], sibling).wait_recv()
    g_ref[...] = gram_row[...].reshape(256, 256)
    for group in range(2):
        for part in range(2):
            for away in FAR_FIRST:
                first_copy(group, part, away).wait_send()
    for copy in sends:
        copy.wait_send()


def exchange(velocity, basis_in):
    rows, snaps = velocity.shape
    rank = basis_in.shape[1]
    f32, bf16 = jnp.float32, jnp.bfloat16

    def pair(*shape):
        return [pltpu.SemaphoreType.DMA(shape)] * 2

    return pl.pallas_call(
        exchange_kernel,
        out_shape=(
            jax.ShapeDtypeStruct((rows, rank), f32),
            jax.ShapeDtypeStruct((rank, rank), f32),
        ),
        in_specs=[pl.BlockSpec(memory_space=pltpu.HBM)] * 2,
        out_specs=[pl.BlockSpec(memory_space=pltpu.VMEM)] * 2,
        scratch_shapes=[
            pltpu.VMEM((rows, snaps), bf16),
            pltpu.VMEM((rows, snaps // 2), bf16),
            pltpu.VMEM((rows, rank), bf16),
            pltpu.VMEM((rows, rank), bf16),
            pltpu.VMEM((2, 2, 4, 4, NZ, PIECE, 128), f32),
            pltpu.VMEM((2, 2, 4, 4, NZ, PIECE, 128), bf16),
            pltpu.VMEM((2, 2, 3, 4, NZ, PIECE, 128), bf16),
            pltpu.VMEM((2, 2, 3, NZ, PIECE, 128), bf16),
            pltpu.VMEM((2, 2, NZ - 1, PIECE, 128), bf16),
            pltpu.VMEM((2, 2, 2, 4, 4, NZ, PIECE, 128), bf16),
            pltpu.VMEM((2, rank, rank), f32),
            pltpu.VMEM((NY, NX, 16, rank), f32),
            pltpu.VMEM((NY * NX - 1, 16, rank), f32),
            pltpu.VMEM((NZ, 16, rank), f32),
            pltpu.VMEM((NY, NX, 16, rank), f32),
            pltpu.SemaphoreType.DMA((10,)),
            *pair(9),
            *pair(2, 2, 3),
            *pair(2, 2, 3),
            *pair(2, 2, NZ - 1),
            *pair(2, 2, NZ - 1),
            *pair(2, 2, 3),
            *pair(2, 2, 3),
            *pair(2, 2, 4),
            *pair(39),
        ],
        compiler_params=pltpu.CompilerParams(
            collective_id=0, has_side_effects=True, vmem_limit_bytes=48 * 2**20
        ),
        cost_estimate=pl.CostEstimate(
            flops=4 * rows * snaps * rank, bytes_accessed=2 * rows * snaps, transcendentals=0
        ),
    )(velocity, basis_in)


def factor_kernel(scale, p_ref, g_ref, out_ref, r_ref, w, state):
    size = g_ref.shape[0]
    row = lax.broadcasted_iota(jnp.int32, (size, size), 0)
    col = lax.broadcasted_iota(jnp.int32, (size, size), 1)
    eye = (row == col).astype(jnp.float32)
    weight = jnp.where(row < col, 1.0, 0.5 * eye)
    gram = g_ref[...]
    diagonal = gram * eye
    unit_row = lax.rsqrt(jnp.sum(diagonal, axis=0, keepdims=True))
    unit_col = lax.rsqrt(jnp.sum(diagonal, axis=1, keepdims=True))
    scaled = gram * unit_row * unit_col

    w[...] = eye
    state[...] = scaled - eye

    def go_on(carry):
        count, norm = carry
        return (norm > 1e-6) & (norm < 1e4) & (count < 12)

    def improve():
        upper = state[...] * weight
        once = dot(w[...], upper, (1, 0), HIGHEST)
        w[...] = w[...] - once + dot(once, upper, (1, 0), HIGHEST)

    def step(carry):
        count, _ = carry
        improve()
        excess = dot(w[...], dot(scaled, w[...], (1, 0), HIGHEST), (0, 0), HIGHEST) - eye
        state[...] = excess
        return count + 1, jnp.sum(excess * excess)

    start = state[...]
    _, norm = lax.while_loop(go_on, step, (0, jnp.sum(start * start)))
    converged = norm <= 1e-6

    @pl.when(converged)
    def _():
        improve()

    @pl.when(jnp.logical_not(converged))
    def _():
        state[...] = scaled
        r_ref[...] = jnp.zeros_like(r_ref)
        lane = lax.broadcasted_iota(jnp.int32, (1, size), 1)

        def eliminate(j, _):
            pivot_row = jnp.where(lane >= j, state[pl.ds(j, 1), :], 0.0)
            pivot = jnp.sum(jnp.where(lane == j, pivot_row, 0.0), axis=1, keepdims=True)
            pivot_row = pivot_row / jnp.sqrt(pivot)
            r_ref[pl.ds(j, 1), :] = pivot_row
            pivot_col = jnp.sum(jnp.broadcast_to(pivot_row, (size, size)) * eye, axis=1, keepdims=True)
            state[...] = state[...] - pivot_col * pivot_row
            return 0

        lax.fori_loop(0, size, eliminate, 0)
        w[...] = jnp.zeros_like(w)

        def substitute(n, _):
            j = size - 1 - n
            line = r_ref[pl.ds(j, 1), :]
            pivot = jnp.sum(jnp.where(lane == j, line, 0.0), axis=1, keepdims=True)
            beyond = jnp.where(lane > j, line, 0.0)
            unit = jnp.where(lane == j, 1.0, 0.0)
            w[pl.ds(j, 1), :] = (unit - dot(beyond, w[...], (1, 0), HIGHEST)) / pivot
            return 0

        lax.fori_loop(0, size, substitute, 0)

    triangle = jnp.where(row <= col, dot(w[...], scaled, (0, 0), HIGHEST), 0.0)
    r_ref[...] = triangle / unit_row / scale
    out_ref[...] = dot(p_ref[...], w[...] * unit_col * scale, (1, 0), HIGHEST)


def factor(projected, gram, scale):
    rank = gram.shape[0]
    return pl.pallas_call(
        functools.partial(factor_kernel, scale),
        out_shape=(
            jax.ShapeDtypeStruct(projected.shape, jnp.float32),
            jax.ShapeDtypeStruct((rank, rank), jnp.float32),
        ),
        scratch_shapes=[pltpu.VMEM((rank, rank), jnp.float32)] * 2,
        compiler_params=pltpu.CompilerParams(vmem_limit_bytes=32 * 2**20),
    )(projected, gram)


def local(velocity, basis_in):
    projected, gram = exchange(velocity, basis_in)
    scale = float(lax.axis_size("rows") * velocity.shape[0]) ** 0.5
    return factor(projected, gram, scale)


def solution(mesh):
    in_specs = (P("rows", None), P("rows", None))
    out_specs = (P("rows", None), P())
    return jax.shard_map(local, mesh=mesh, in_specs=in_specs, out_specs=out_specs, check_vma=False)
```

time: 102 us -> 92.6 us (0.908)
  Pallas kernels: 100 us -> 90.5 us
    pallas_call x1, Pallas kernels: 90.5 us -> 80.7 us  [exchange(): pl.pallas_call(exchange_kernel, out_shape=(jax.ShapeDtypeStruct((rows, ra...]
where the time goes in v3:
time: 92.6 us; the launch traced here: 92.1 us
  Pallas kernels  90.5 us (98%)
  local copies, waits for them, and re-layouts  0.94 us (1%)
    pallas_call x1, Pallas kernels, exchange(): pl.pallas_call(exchange_kernel, out_shape=(jax.ShapeDtypeStruct((rows, ra...  80.7 us
    pallas_call x1, Pallas kernels, factor(): pl.pallas_call(functools.partial(factor_kernel, scale), out_shape=(jax.Sh...  9.79 us

profile of v3, /device:TPU:1, one launch (start us, length us, event | category | flops | bytes accessed | tf_op | source)
XLA Modules:
  0.0 92.1 jit_solution(13745274977293058084)
XLA Ops:
  0.6 0.0 copy-start
  0.6 0.9 %copy-done = bf16[512,256]{1,0:T(8,128)(2,1)S(1)} copy-done((bf16[512,256]{1,0:T(8,128)(2,1)S(1)}, bf16[512,256]{1,0:T(8,128)(2,1)}, u32[]{:S(2)}) %copy-start) | copy-done | bytes 262168
  1.6 80.7 %shard_map.41 = (f32[512,256]{1,0:T(8,128)S(1)}, f32[256,256]{1,0:T(8,128)S(1)}) custom-call(bf16[512,8192]{1,0:T(8,128)(2,1)} %v_hbm.1, bf16[512,256]{1,0:T(8,128)(2,1)S(1)} %copy-done), custom_call_target="tpu_custom_call" | custom-call | flops 4294967296 | bytes 8388608 | tf_op jit(solution)/shard_map/pallas_call | solution.py:354
  82.3 9.8 %shard_map.42 = (f32[512,256]{1,0:T(8,128)}, f32[256,256]{1,0:T(8,128)}) custom-call(f32[512,256]{1,0:T(8,128)S(1)} %get-tuple-element.4.p_ref, f32[256,256]{1,0:T(8,128)S(1)} %get-tuple-element.5.g_ref), custom_call_target="tpu_custom_call" | custom-call | tf_op jit(solution)/shard_map/pallas_call | solution.py:473
Async XLA Ops:
  0.6 1.0 %copy-start = (bf16[512,256]{1,0:T(8,128)(2,1)S(1)}, bf16[512,256]{1,0:T(8,128)(2,1)}, u32[]{:S(2)}) copy-start(bf16[512,256]{1,0:T(8,128)(2,1)} %b_hbm.1) | copy-start | bytes 786436

commit v4 on v3

--- a/solution.py
+++ b/solution.py
@@ -43,10 +43,10 @@
 
 
 def exchange_kernel(
-    v_hbm, b_hbm, p_ref, g_ref,
-    v, v_sib, b, b_sib, total, coded, in_first, in_second, in_z, gathered,
+    v_hbm, b_hbm, p_hbm, g_ref,
+    p_ref, v, v_sib, b, b_sib, early, total, coded, in_far, in_near, in_second, in_z, gathered,
     gram_in, gram_chip, gram_parts, gram_z, gram_row,
-    load_sem, sib_send, sib_recv, first_send, first_recv, second_send, second_recv,
+    load_sem, sib_send, sib_recv, far_send, far_recv, near_send, near_recv, second_send, second_recv,
     z_send, z_recv, out_z_send, out_z_recv, out_second_send, out_second_recv,
     out_first_send, out_first_recv, fwd_send, fwd_recv, gx_send, gx_recv,
 ):
@@ -81,7 +81,11 @@
     def columns(which_core, group, k):
         return pl.ds(pl.multiple_of(which_core * half + (2 * k + group) * wide, 128), wide)
 
-    order = [(group, along("x", offset)) for group in range(2) for offset in FAR_FIRST + (0,)]
+    apart = (mine["y"] - mine["x"] + 4) % 4
+    same, three = 1 - (apart + 3) // 4, apart % 2 * (apart // 2)
+    one, two = apart % 2 * (1 - apart // 2), (1 - apart % 2) * (apart // 2)
+    offsets = (2, same + 3 * one + three, 3 * same + one + two + 3 * three, 3 * two)
+    order = [(group, along("x", offset)) for group in range(2) for offset in offsets]
     loads = []
     for group, k in order:
         loads.append(pltpu.make_async_copy(
@@ -103,6 +107,12 @@
     barrier = pltpu.get_barrier_semaphore()
     for partner in partners:
         pl.semaphore_signal(barrier, inc=1, device_id=partner, device_id_type=MESH)
+
+    load_b.wait()
+    b_t = b[...].T
+    for n in range(4):
+        loads[n].wait()
+        early[n] = dot(b_t, v[:, columns(core, *order[n])], (1, 0))
     pl.semaphore_wait(barrier, len(partners))
 
     copy_b = remote(b_hbm, b_sib, sib_send.at[8], sib_recv.at[8], sibling)
@@ -115,22 +125,40 @@
         start(copy)
         copies_v.append(copy)
 
-    load_b.wait()
-    b_t = b[...].T
     copy_b.wait_recv()
     b_sib_t = b_sib[...].T
 
-    def first_copy(group, part, away):
+    def far_copy(group, part, way):
         first, _ = PARTS[part]
-        k = along(first, away)
         return remote(
-            coded.at[group, part, k], in_first.at[group, part, away - 1],
-            first_send.at[group, part, away - 1], first_recv.at[group, part, away - 1], device(**{first: k}))
+            coded.at[group, part, along(first, 2), pl.ds(2 * way, 2)], in_far.at[group, part, way],
+            far_send.at[group, part, way], far_recv.at[group, part, way],
+            device(**{first: along(first, 1 - 2 * way)}))
+
+    def near_copy(group, part, way, relay):
+        first, _ = PARTS[part]
+        k = along(first, 1 - 2 * way)
+        half_of = pl.ds(2 * way if relay else 2 - 2 * way, 2)
+        slot = 2 * way + relay
+        return remote(
+            coded.at[group, part, k, half_of], in_near.at[group, part, way, half_of],
+            near_send.at[group, part, slot], near_recv.at[group, part, slot], device(**{first: k}))
+
+    def relay(group):
+        for part, (first, _) in enumerate(PARTS):
+            for way in range(2):
+                far_copy(group, part, way).wait_recv()
+                at = (group, part, along(first, 1 - 2 * way), pl.ds(2 * way, 2))
+                coded[at] = encode(total[at] + decode(in_far[group, part, way]))
+                near_copy(group, part, way, 1).start()
 
     for n, (group, k) in enumerate(order):
-        loads[n].wait()
+        if group:
+            loads[n].wait()
+            product = dot(b_t, v[:, columns(core, group, k)], (1, 0))
+        else:
+            product = early[n]
         copies_v[n].wait_recv()
-        product = dot(b_t, v[:, columns(core, group, k)], (1, 0))
         product += dot(b_sib_t, v_sib[:, n * wide:(n + 1) * wide], (1, 0))
         for part in range(2):
             for z in range(NZ):
@@ -139,23 +167,31 @@
                     tile = product[rank:rank + PIECE, z // 2 * 128:(z // 2 + 1) * 128]
                     total[group, part, k, o2, z] = tile
                     coded[group, part, k, o2, z] = encode(tile)
-        if n % 4 < 3:
-            first_copy(group, 0, FAR_FIRST[n % 4]).start()
-        away = (k - mine["y"] + NY) % NY
-
-        @pl.when(away != 0)
-        def _():
-            first_copy(group, 1, away).start()
+        for part, (first, _) in enumerate(PARTS):
+            away = (k - mine[first] + 4) % 4
+
+            @pl.when(away == 2)
+            def _():
+                for way in range(2):
+                    far_copy(group, part, way).start()
+
+            @pl.when(away % 2 == 1)
+            def _():
+                near_copy(group, part, away // 2, 0).start()
+        if n == 5:
+            relay(0)
+    relay(1)
 
     def sum_first(group):
         for part, (first, second) in enumerate(PARTS):
-            for away in FAR_FIRST:
-                first_copy(group, part, away).wait_recv()
+            for way in range(2):
+                for kind in range(2):
+                    near_copy(group, part, way, kind).wait_recv()
             for j2 in FAR_FIRST + (0,):
                 o2 = along(second, j2)
                 block = total[group, part, mine[first], o2]
-                for away in FAR_FIRST:
-                    block += decode(in_first[group, part, away - 1, o2])
+                for way in range(2):
+                    block += decode(in_near[group, part, way, o2])
                 if j2:
                     coded[group, part, mine[first], o2] = encode(block)
                     start(remote(
@@ -293,6 +329,8 @@
     from_sibling(1, 2)
 
     projected = p_ref[...]
+    store = pltpu.make_async_copy(p_ref, p_hbm, load_sem.at[10])
+    store.start()
     gram_in[0] = dot(projected, projected, (0, 0), HIGHEST)
 
     copy = remote(gram_in.at[0], gram_in.at[1], gx_send.at[0], gx_recv.at[0], sibling)
@@ -335,10 +373,13 @@
         there = gram_row.at[along("y", -dy), along("x", -dx)]
         remote(there, there, gx_send.at[slot], gx_recv.at[slot], sibling).wait_recv()
     g_ref[...] = gram_row[...].reshape(256, 256)
+    store.wait()
     for group in range(2):
         for part in range(2):
-            for away in FAR_FIRST:
-                first_copy(group, part, away).wait_send()
+            for way in range(2):
+                far_copy(group, part, way).wait_send()
+                for kind in range(2):
+                    near_copy(group, part, way, kind).wait_send()
     for copy in sends:
         copy.wait_send()
 
@@ -358,15 +399,18 @@
             jax.ShapeDtypeStruct((rank, rank), f32),
         ),
         in_specs=[pl.BlockSpec(memory_space=pltpu.HBM)] * 2,
-        out_specs=[pl.BlockSpec(memory_space=pltpu.VMEM)] * 2,
+        out_specs=[pl.BlockSpec(memory_space=pl.ANY), pl.BlockSpec(memory_space=pltpu.VMEM)],
         scratch_shapes=[
+            pltpu.VMEM((rows, rank), f32),
             pltpu.VMEM((rows, snaps), bf16),
             pltpu.VMEM((rows, snaps // 2), bf16),
             pltpu.VMEM((rows, rank), bf16),
             pltpu.VMEM((rows, rank), bf16),
+            pltpu.VMEM((4, rank, snaps // 16), f32),
             pltpu.VMEM((2, 2, 4, 4, NZ, PIECE, 128), f32),
             pltpu.VMEM((2, 2, 4, 4, NZ, PIECE, 128), bf16),
-            pltpu.VMEM((2, 2, 3, 4, NZ, PIECE, 128), bf16),
+            pltpu.VMEM((2, 2, 2, 2, NZ, PIECE, 128), bf16),
+            pltpu.VMEM((2, 2, 2, 4, NZ, PIECE, 128), bf16),
             pltpu.VMEM((2, 2, 3, NZ, PIECE, 128), bf16),
             pltpu.VMEM((2, 2, NZ - 1, PIECE, 128), bf16),
             pltpu.VMEM((2, 2, 2, 4, 4, NZ, PIECE, 128), bf16),
@@ -375,9 +419,10 @@
             pltpu.VMEM((NY * NX - 1, 16, rank), f32),
             pltpu.VMEM((NZ, 16, rank), f32),
             pltpu.VMEM((NY, NX, 16, rank), f32),
-            pltpu.SemaphoreType.DMA((10,)),
+            pltpu.SemaphoreType.DMA((11,)),
             *pair(9),
-            *pair(2, 2, 3),
+            *pair(2, 2, 2),
+            *pair(2, 2, 4),
             *pair(2, 2, 3),
             *pair(2, 2, NZ - 1),
             *pair(2, 2, NZ - 1),
@@ -387,7 +432,7 @@
             *pair(39),
         ],
         compiler_params=pltpu.CompilerParams(
-            collective_id=0, has_side_effects=True, vmem_limit_bytes=48 * 2**20
+            collective_id=0, has_side_effects=True, vmem_limit_bytes=107 * 2**19
         ),
         cost_estimate=pl.CostEstimate(
             flops=4 * rows * snaps * rank, bytes_accessed=2 * rows * snaps, transcendentals=0
@@ -395,8 +440,18 @@
     )(velocity, basis_in)
 
 
-def factor_kernel(scale, p_ref, g_ref, out_ref, r_ref, w, state):
+def split_dot(a, b):
+    a_high, b_high = a.astype(jnp.bfloat16), b.astype(jnp.bfloat16)
+    a_low = (a - a_high.astype(jnp.float32)).astype(jnp.bfloat16)
+    b_low = (b - b_high.astype(jnp.float32)).astype(jnp.bfloat16)
+    return dot(a_high, b_high, (1, 0)) + (dot(a_high, b_low, (1, 0)) + dot(a_low, b_high, (1, 0)))
+
+
+def factor_kernel(scale, p_hbm, g_ref, out_hbm, r_hbm, p_ref, out, r_ref, moved, state, sem):
+    load = pltpu.make_async_copy(p_hbm, p_ref, sem.at[5])
+    load.start()
     size = g_ref.shape[0]
+    bf16 = jnp.bfloat16
     row = lax.broadcasted_iota(jnp.int32, (size, size), 0)
     col = lax.broadcasted_iota(jnp.int32, (size, size), 1)
     eye = (row == col).astype(jnp.float32)
@@ -406,33 +461,55 @@
     unit_row = lax.rsqrt(jnp.sum(diagonal, axis=0, keepdims=True))
     unit_col = lax.rsqrt(jnp.sum(diagonal, axis=1, keepdims=True))
     scaled = gram * unit_row * unit_col
-
-    w[...] = eye
-    state[...] = scaled - eye
+    excess = scaled - eye
+
+    def refine(u):
+        small = u.astype(bf16)
+        return u - weight * dot(small, small, (0, 0))
+
+    def advance(d, u, exact):
+        x = refine(u) if exact else u
+        small = x.astype(bf16)
+        y = x - dot(small, small, (1, 0))
+        if exact:
+            return d - y - dot(d, y, (1, 0), HIGHEST)
+        return d - y - dot(d.astype(bf16), y.astype(bf16), (1, 0))
+
+    def rest(d, exact):
+        if exact:
+            once = excess + dot(excess, d, (1, 0), HIGHEST)
+            return weight * (once + dot(d, d + once, (0, 0), HIGHEST)) + d
+        near = d.astype(bf16)
+        once = excess + dot(excess.astype(bf16), near, (1, 0))
+        return weight * (once + dot(near, (d + once).astype(bf16), (0, 0))) + d
+
+    x = refine(weight * excess)
+    small = x.astype(bf16)
+    square = dot(small, small, (1, 0))
+    d = square - x - dot(square.astype(bf16), small, (1, 0))
+    d = advance(d, rest(d, False), False)
+    u = rest(d, True)
+    moved[...] = d
+    state[...] = u
 
     def go_on(carry):
         count, norm = carry
-        return (norm > 1e-6) & (norm < 1e4) & (count < 12)
-
-    def improve():
-        upper = state[...] * weight
-        once = dot(w[...], upper, (1, 0), HIGHEST)
-        w[...] = w[...] - once + dot(once, upper, (1, 0), HIGHEST)
+        return (norm > 2e-5) & (norm < 1e4) & (count < 12)
 
     def step(carry):
         count, _ = carry
-        improve()
-        excess = dot(w[...], dot(scaled, w[...], (1, 0), HIGHEST), (0, 0), HIGHEST) - eye
-        state[...] = excess
-        return count + 1, jnp.sum(excess * excess)
-
-    start = state[...]
-    _, norm = lax.while_loop(go_on, step, (0, jnp.sum(start * start)))
-    converged = norm <= 1e-6
+        d = advance(moved[...], state[...], True)
+        u = rest(d, True)
+        moved[...] = d
+        state[...] = u
+        return count + 1, jnp.sum(u * u)
+
+    _, norm = lax.while_loop(go_on, step, (0, jnp.sum(u * u)))
+    converged = norm <= 2e-5
 
     @pl.when(converged)
     def _():
-        improve()
+        moved[...] = advance(moved[...], state[...], True)
 
     @pl.when(jnp.logical_not(converged))
     def _():
@@ -450,7 +527,7 @@
             return 0
 
         lax.fori_loop(0, size, eliminate, 0)
-        w[...] = jnp.zeros_like(w)
+        moved[...] = jnp.zeros_like(moved)
 
         def substitute(n, _):
             j = size - 1 - n
@@ -458,14 +535,30 @@
             pivot = jnp.sum(jnp.where(lane == j, line, 0.0), axis=1, keepdims=True)
             beyond = jnp.where(lane > j, line, 0.0)
             unit = jnp.where(lane == j, 1.0, 0.0)
-            w[pl.ds(j, 1), :] = (unit - dot(beyond, w[...], (1, 0), HIGHEST)) / pivot
+            moved[pl.ds(j, 1), :] = (unit - dot(beyond, moved[...], (1, 0), HIGHEST)) / pivot
             return 0
 
         lax.fori_loop(0, size, substitute, 0)
-
-    triangle = jnp.where(row <= col, dot(w[...], scaled, (0, 0), HIGHEST), 0.0)
-    r_ref[...] = triangle / unit_row / scale
-    out_ref[...] = dot(p_ref[...], w[...] * unit_col * scale, (1, 0), HIGHEST)
+        moved[...] = moved[...] - eye
+
+    d = moved[...]
+    load.wait()
+    copies = []
+    rows = p_ref.shape[0] // 4
+    for n in range(4):
+        block = pl.ds(n * rows, rows)
+        p = p_ref[block, :] * (unit_row * scale)
+        out[block, :] = p + split_dot(p, d)
+        copy = pltpu.make_async_copy(out.at[block, :], out_hbm.at[block, :], sem.at[n])
+        copy.start()
+        copies.append(copy)
+    triangle = jnp.where(row <= col, scaled + dot(d, scaled, (0, 0), HIGHEST), 0.0)
+    r_ref[...] = triangle / (unit_row * scale)
+    copy = pltpu.make_async_copy(r_ref, r_hbm, sem.at[4])
+    copy.start()
+    copies.append(copy)
+    for copy in copies:
+        copy.wait()
 
 
 def factor(projected, gram, scale):
@@ -476,8 +569,14 @@
             jax.ShapeDtypeStruct(projected.shape, jnp.float32),
             jax.ShapeDtypeStruct((rank, rank), jnp.float32),
         ),
-        scratch_shapes=[pltpu.VMEM((rank, rank), jnp.float32)] * 2,
-        compiler_params=pltpu.CompilerParams(vmem_limit_bytes=32 * 2**20),
+        in_specs=[pl.BlockSpec(memory_space=pl.ANY), pl.BlockSpec(memory_space=pltpu.VMEM)],
+        out_specs=[pl.BlockSpec(memory_space=pl.ANY)] * 2,
+        scratch_shapes=[
+            *[pltpu.VMEM(projected.shape, jnp.float32)] * 2,
+            *[pltpu.VMEM((rank, rank), jnp.float32)] * 3,
+            pltpu.SemaphoreType.DMA((6,)),
+        ],
+        compiler_params=pltpu.CompilerParams(vmem_limit_bytes=107 * 2**19),
     )(projected, gram)
 
 

time: 92.6 us -> 87.4 us (0.944)
  Pallas kernels: 90.5 us -> 85.4 us
  local copies, waits for them, and re-layouts: 0.94 us -> 0 us
    pallas_call x1, Pallas kernels: 9.79 us -> 6.81 us  [factor(): pl.pallas_call(functools.partial(factor_kernel, scale), out_shape=(jax.Sh...]
    pallas_call x1, Pallas kernels: 80.7 us -> 78.6 us  [exchange(): pl.pallas_call(exchange_kernel, out_shape=(jax.ShapeDtypeStruct((rows, ra...]
    unnamed x2 -> x0, local copies, waits for them, and re-layouts: 0.94 us -> none
where the time goes in v4:
time: 87.4 us; the launch traced here: 86.2 us
  Pallas kernels  85.4 us (98%)
    pallas_call x1, Pallas kernels, exchange(): pl.pallas_call(exchange_kernel, out_shape=(jax.ShapeDtypeStruct((rows, ra...  78.6 us
    pallas_call x1, Pallas kernels, factor(): pl.pallas_call(functools.partial(factor_kernel, scale), out_shape=(jax.Sh...  6.81 us

profile of v4, /device:TPU:1, one launch (start us, length us, event | category | flops | bytes accessed | tf_op | source)
XLA Modules:
  0.0 86.2 jit_solution(18243057182322827194)
XLA Ops:
  0.6 78.6 %shard_map.41 = (f32[512,256]{1,0:T(8,128)}, f32[256,256]{1,0:T(8,128)S(1)}) custom-call(bf16[512,8192]{1,0:T(8,128)(2,1)} %v_hbm.1, bf16[512,256]{1,0:T(8,128)(2,1)} %b_hbm.1), custom_call_target="tpu_custom_call" | custom-call | flops 4294967296 | bytes 8388608 | tf_op jit(solution)/shard_map/pallas_call | solution.py:395
  79.3 6.8 %shard_map.42 = (f32[512,256]{1,0:T(8,128)}, f32[256,256]{1,0:T(8,128)}) custom-call(f32[512,256]{1,0:T(8,128)} %get-tuple-element.4.p_hbm, f32[256,256]{1,0:T(8,128)S(1)} %get-tuple-element.5.g_ref), custom_call_target="tpu_custom_call" | custom-call | tf_op jit(solution)/shard_map/pallas_call | solution.py:566

commit v5 on v4

--- a/solution.py
+++ b/solution.py
@@ -107,12 +107,6 @@
     barrier = pltpu.get_barrier_semaphore()
     for partner in partners:
         pl.semaphore_signal(barrier, inc=1, device_id=partner, device_id_type=MESH)
-
-    load_b.wait()
-    b_t = b[...].T
-    for n in range(4):
-        loads[n].wait()
-        early[n] = dot(b_t, v[:, columns(core, *order[n])], (1, 0))
     pl.semaphore_wait(barrier, len(partners))
 
     copy_b = remote(b_hbm, b_sib, sib_send.at[8], sib_recv.at[8], sibling)
@@ -125,6 +119,11 @@
         start(copy)
         copies_v.append(copy)
 
+    load_b.wait()
+    b_t = b[...].T
+    for n in range(4):
+        loads[n].wait()
+        early[n] = dot(b_t, v[:, columns(core, *order[n])], (1, 0))
     copy_b.wait_recv()
     b_sib_t = b_sib[...].T
 
@@ -311,22 +310,22 @@
     loads[8].wait()
     from_chip(0, 0)
     spread_second(1)
+    from_sibling(0, 0)
+    from_chip(0, 2)
+    spread_first(1)
     from_chip(0, 1)
-    from_sibling(0, 0)
-    spread_first(1)
+    from_sibling(0, 2)
     from_chip(0, 3)
     from_chip(1, 0)
     from_sibling(0, 1)
-    from_chip(0, 2)
     from_sibling(0, 3)
     from_sibling(1, 0)
+    from_chip(1, 2)
     from_chip(1, 1)
-    from_sibling(0, 2)
+    from_sibling(1, 2)
     from_chip(1, 3)
     from_sibling(1, 1)
-    from_chip(1, 2)
     from_sibling(1, 3)
-    from_sibling(1, 2)
 
     projected = p_ref[...]
     store = pltpu.make_async_copy(p_ref, p_hbm, load_sem.at[10])

time: 87.4 us -> 86 us (0.984)
  no operation moved by 1% of the time
where the time goes in v5:
time: 86 us; the launch traced here: 85.5 us
  Pallas kernels  84.7 us (98%)
    pallas_call x1, Pallas kernels, exchange(): pl.pallas_call(exchange_kernel, out_shape=(jax.ShapeDtypeStruct((rows, ra...  77.8 us
    pallas_call x1, Pallas kernels, factor(): pl.pallas_call(functools.partial(factor_kernel, scale), out_shape=(jax.Sh...  6.97 us

profile of v5, /device:TPU:1, one launch (start us, length us, event | category | flops | bytes accessed | tf_op | source)
XLA Modules:
  0.0 85.5 jit_solution(2388352544355310886)
XLA Ops:
  0.6 77.8 %shard_map.41 = (f32[512,256]{1,0:T(8,128)}, f32[256,256]{1,0:T(8,128)S(1)}) custom-call(bf16[512,8192]{1,0:T(8,128)(2,1)} %v_hbm.1, bf16[512,256]{1,0:T(8,128)(2,1)} %b_hbm.1), custom_call_target="tpu_custom_call" | custom-call | flops 4294967296 | bytes 8388608 | tf_op jit(solution)/shard_map/pallas_call | solution.py:394
  78.4 7.0 %shard_map.42 = (f32[512,256]{1,0:T(8,128)}, f32[256,256]{1,0:T(8,128)}) custom-call(f32[512,256]{1,0:T(8,128)} %get-tuple-element.4.p_hbm, f32[256,256]{1,0:T(8,128)S(1)} %get-tuple-element.5.g_ref), custom_call_target="tpu_custom_call" | custom-call | tf_op jit(solution)/shard_map/pallas_call | solution.py:565

commit v6 on v5

--- a/solution.py
+++ b/solution.py
@@ -74,6 +74,11 @@
     def start(copy):
         copy.start()
         sends.append(copy)
+
+    def settle():
+        for copy in sends:
+            copy.wait_send()
+        sends.clear()
 
     half = v_sib.shape[1]
     wide = half // (2 * NX)
@@ -343,8 +348,17 @@
         y, x = along("y", dy), along("x", dx)
         copy = remote(
             gram_chip.at[y, x], gram_parts.at[n], gx_send.at[1 + n], gx_recv.at[1 + n], device(y=y, x=x))
-        start(copy)
+        copy.start()
         scatter.append(copy)
+
+    for group in range(2):
+        for part in range(2):
+            for way in range(2):
+                far_copy(group, part, way).wait_send()
+                for kind in range(2):
+                    near_copy(group, part, way, kind).wait_send()
+    settle()
+    store.wait()
     row = gram_chip[mine["y"], mine["x"]]
     for n, copy in reversed(list(enumerate(scatter))):
         copy.wait_recv()
@@ -354,10 +368,13 @@
         slot = 16 + dz
         here = gram_z.at[mine["z"]]
         start(remote(here, here, gx_send.at[slot], gx_recv.at[slot], device(z=along("z", dz))))
+    for copy in scatter:
+        copy.wait_send()
     for dz in Z_NEAR_FIRST:
         slot = 16 + dz
         there = gram_z.at[along("z", -dz)]
         remote(there, there, gx_send.at[slot], gx_recv.at[slot], sibling).wait_recv()
+    settle()
     row = gram_z[0]
     for n in range(1, NZ):
         row += gram_z[n]
@@ -372,15 +389,7 @@
         there = gram_row.at[along("y", -dy), along("x", -dx)]
         remote(there, there, gx_send.at[slot], gx_recv.at[slot], sibling).wait_recv()
     g_ref[...] = gram_row[...].reshape(256, 256)
-    store.wait()
-    for group in range(2):
-        for part in range(2):
-            for way in range(2):
-                far_copy(group, part, way).wait_send()
-                for kind in range(2):
-                    near_copy(group, part, way, kind).wait_send()
-    for copy in sends:
-        copy.wait_send()
+    settle()
 
 
 def exchange(velocity, basis_in):

time: 86 us -> 85.8 us (level)
  no operation moved by 1% of the time
where the time goes in v6:
time: 85.8 us; the launch traced here: 85.3 us
  Pallas kernels  84.5 us (98%)
    pallas_call x1, Pallas kernels, exchange(): pl.pallas_call(exchange_kernel, out_shape=(jax.ShapeDtypeStruct((rows, ra...  77.5 us
    pallas_call x1, Pallas kernels, factor(): pl.pallas_call(functools.partial(factor_kernel, scale), out_shape=(jax.Sh...  6.99 us

profile of v6, /device:TPU:1, one launch (start us, length us, event | category | flops | bytes accessed | tf_op | source)
XLA Modules:
  0.0 85.3 jit_solution(16286278005148731681)
XLA Ops:
  0.6 77.5 %shard_map.41 = (f32[512,256]{1,0:T(8,128)}, f32[256,256]{1,0:T(8,128)S(1)}) custom-call(bf16[512,8192]{1,0:T(8,128)(2,1)} %v_hbm.1, bf16[512,256]{1,0:T(8,128)(2,1)} %b_hbm.1), custom_call_target="tpu_custom_call" | custom-call | flops 4294967296 | bytes 8388608 | tf_op jit(solution)/shard_map/pallas_call | solution.py:403
  78.1 7.0 %shard_map.42 = (f32[512,256]{1,0:T(8,128)}, f32[256,256]{1,0:T(8,128)}) custom-call(f32[512,256]{1,0:T(8,128)} %get-tuple-element.4.p_hbm, f32[256,256]{1,0:T(8,128)S(1)} %get-tuple-element.5.g_ref), custom_call_target="tpu_custom_call" | custom-call | tf_op jit(solution)/shard_map/pallas_call | solution.py:574
